TPU v7x, 32 devices: a whole 2x2x4 slice. The times are simulated.
32 devices in a mesh: ctx: 16 (over z, y, x), wa: 2 (over core).
Axes of the slice: x: 2, y: 2, z: 4, core: 2. Of those that a mesh axis runs over, the one named last changes fastest.
Arguments:
- tokens: bfloat16 [4096, 768], P('ctx'), may hold values from -6 to 6
- cotangent: bfloat16 [4096, 768], P('ctx'), may hold values from -6 to 6
- routes: int32 [4096, 2], P('ctx'), may hold values from 0 to 15, all different within a row; in each aligned block of 256 rows (0 to 255, 256 to 511, ...) at most 64 rows name the same one
- buckets: int32 [1024], replicated, may hold values from 0 to 31
- block_order: int32 [16], replicated, may hold values from 0 to 15, each once
- attend_gain1: float32 [768], replicated, may hold values from 0.5 to 1.5
- rel_bias1: float32 [12, 32], P('wa'), may hold values from -4 to 4
- query_proj1: bfloat16 [768, 768], P('ctx', 'wa'), may hold values from -0.21875 to 0.21875
- key_proj1: bfloat16 [768, 768], P('ctx', 'wa'), may hold values from -0.21875 to 0.21875
- value_proj1: bfloat16 [768, 768], P('ctx', 'wa'), may hold values from -0.21875 to 0.21875
- output_proj1: bfloat16 [768, 768], P('ctx', 'wa'), may hold values from -0.625 to 0.625
- dense_gain1: float32 [768], replicated, may hold values from 0.5 to 1.5
- dense_up1: bfloat16 [768, 3072], P('ctx', 'wa'), may hold values from -0.21875 to 0.21875
- dense_down1: bfloat16 [768, 3072], P('ctx', 'wa'), may hold values from -0.109375 to 0.109375
- attend_gain2: float32 [768], replicated, may hold values from 0.5 to 1.5
- rel_bias2: float32 [12, 32], P('wa'), may hold values from -4 to 4
- query_proj2: bfloat16 [768, 768], P('ctx', 'wa'), may hold values from -0.21875 to 0.21875
- key_proj2: bfloat16 [768, 768], P('ctx', 'wa'), may hold values from -0.21875 to 0.21875
- value_proj2: bfloat16 [768, 768], P('ctx', 'wa'), may hold values from -0.21875 to 0.21875
- output_proj2: bfloat16 [768, 768], P('ctx', 'wa'), may hold values from -0.625 to 0.625
- expert_gain2: float32 [768], replicated, may hold values from 0.5 to 1.5
- router: float32 [768, 16], replicated, may hold values from -0.21875 to 0.21875
- expert_up: bfloat16 [16, 768, 3072], P('ctx', None, 'wa'), may hold values from -0.21875 to 0.21875
- expert_down: bfloat16 [16, 3072, 768], P('ctx', 'wa'), may hold values from -0.109375 to 0.109375
Outputs:
- result: bfloat16 [4096, 768], P('ctx')
- grad_tokens: float32 [4096, 768], P('ctx')
- grad_attend_gain1: float32 [768], replicated
- grad_rel_bias1: float32 [12, 32], P('wa')
- grad_query_proj1: float32 [768, 768], P('ctx', 'wa')
- grad_key_proj1: float32 [768, 768], P('ctx', 'wa')
- grad_value_proj1: float32 [768, 768], P('ctx', 'wa')
- grad_output_proj1: float32 [768, 768], P('ctx', 'wa')
- grad_dense_gain1: float32 [768], replicated
- grad_dense_up1: float32 [768, 3072], P('ctx', 'wa')
- grad_dense_down1: float32 [768, 3072], P('ctx', 'wa')
- grad_attend_gain2: float32 [768], replicated
- grad_rel_bias2: float32 [12, 32], P('wa')
- grad_query_proj2: float32 [768, 768], P('ctx', 'wa')
- grad_key_proj2: float32 [768, 768], P('ctx', 'wa')
- grad_value_proj2: float32 [768, 768], P('ctx', 'wa')
- grad_output_proj2: float32 [768, 768], P('ctx', 'wa')
- grad_expert_gain2: float32 [768], replicated
- grad_router: float32 [768, 16], replicated
- grad_expert_up: float32 [16, 768, 3072], P('ctx', None, 'wa')
- grad_expert_down: float32 [16, 3072, 768], P('ctx', 'wa')
Inputs may be any that keep to these rules, and one draw needn't show every extreme that they name: `routes`: the 2 experts of a token differ. Among the 256 rows of one index of ctx no expert is named more than 64 times, a bound that some block reaches. `block_order`: each block position appears once.
All inputs are finite; a program needn't handle non-finite values.
Results may differ from a plain program's by a relative error of at most 0.029.
Values may be sent and summed in bfloat16 or wider, within the bound.
A program may use at most 448 MiB of HBM per device.

v0:
```python
import jax
import jax.numpy as jnp
from jax import lax
from jax.sharding import PartitionSpec as P

HS = 64
SEQS = 4
BLK = 64


HIGHEST = lax.Precision.HIGHEST
epsilon = 1e-06
masked_value = -1e30


def cut_along(array, dim, size):
    before, after = (array.shape[:dim], array.shape[dim + 1 :])
    return jnp.moveaxis(array.reshape(*before, size, -1, *after), dim, 0)


def sum_at_owner(array, axis, dim):
    size = lax.axis_size(axis)
    parts = lax.all_to_all(cut_along(array, dim, size), axis, 0, 0, tiled=True)
    return jnp.sum(parts.astype(jnp.float32), axis=0)


def sent_together(arrays, axis, dim, along):
    ends, at = ([], 0)
    for a in arrays[:-1]:
        at += a.shape[along]
        ends.append(at)
    both = jnp.concatenate(arrays, axis=along)
    return tuple(jnp.split(sum_at_owner(both, axis, dim), ends, axis=along))


def gelu_fn(values):
    return jax.nn.gelu(values, approximate=True)


def rms_norm(inputs, gain):
    inv_rms = lax.rsqrt(jnp.mean(inputs * inputs, axis=-1, keepdims=True) + epsilon)
    return (inputs * inv_rms * gain, inv_rms)


def norm_back(inputs, inv_rms, gain, grad_normed):
    weighted = grad_normed * gain
    gain_grad = jnp.sum(grad_normed * inputs * inv_rms, axis=0)
    grad_inputs = inv_rms * weighted - inputs * inv_rms * inv_rms * inv_rms * jnp.mean(
        weighted * inputs, axis=-1, keepdims=True
    )
    return (grad_inputs, gain_grad)


def half_total(partial_value):
    return lax.psum(partial_value.astype(jnp.bfloat16), "wa").astype(jnp.float32)


def gather_attention(weights):
    return (
        lax.all_gather(weights[0], "ctx", axis=0, tiled=True),
        lax.all_gather(weights[1], "ctx", axis=0, tiled=True),
        lax.all_gather(weights[2], "ctx", axis=0, tiled=True),
        lax.all_gather(weights[3], "ctx", axis=0, tiled=True),
    )


def scatter_attention(grads):
    return sent_together(
        (
            grads[0].astype(jnp.bfloat16),
            grads[1].astype(jnp.bfloat16),
            grads[2].astype(jnp.bfloat16),
            grads[3].astype(jnp.bfloat16),
        ),
        "ctx",
        0,
        1,
    )


def bias_tables(rel_local, buckets):
    seq_len = buckets.shape[0]
    head_count, bucket_count = rel_local.shape
    bucket_table = (buckets[:, None] == jnp.arange(bucket_count, dtype=jnp.int32)[None, :]).astype(
        jnp.float32
    )
    by_distance = jnp.dot(rel_local, bucket_table.T, precision=HIGHEST)
    padded = jnp.concatenate(
        [jnp.zeros((head_count, seq_len - 1), jnp.float32), by_distance], axis=1
    )
    hot_padded = jnp.concatenate(
        [jnp.zeros((seq_len - 1, bucket_count), jnp.float32), bucket_table], axis=0
    )
    return (padded, padded[:, ::-1], hot_padded[::-1])


def skew_rows(window, rows, length):
    head_count, width = window.shape
    tiled = jnp.tile(window, (1, rows + 1))
    return tiled[:, : rows * (width + 1)].reshape(head_count, rows, width + 1)[:, :, :length]


def skew_sum(grid):
    head_count, rows, length = grid.shape
    width = length + rows - 1
    padded = jnp.pad(grid, ((0, 0), (0, 0), (0, rows)))
    return jnp.sum(
        padded.reshape(head_count, -1)[:, : rows * width].reshape(head_count, rows, width), axis=1
    )


def window_start(layout):
    own_block, own_pos, all_pos, perm = layout
    return all_pos.shape[0] - BLK - own_block * BLK


def query_bias(tables, layout):
    own_block, own_pos, all_pos, perm = layout
    table_rev = tables[1]
    head_count = table_rev.shape[0]
    seq_len = all_pos.shape[0]
    num_blocks = perm.shape[0]
    window = lax.dynamic_slice_in_dim(table_rev, window_start(layout), seq_len + BLK - 1, 1)
    ordered = skew_rows(window, BLK, seq_len)[:, ::-1, :].reshape(head_count, BLK, num_blocks, BLK)
    placed = jnp.einsum("hjbi,cb->hjci", ordered, perm, precision=HIGHEST).reshape(
        head_count, BLK, seq_len
    )
    return jnp.where((own_pos[:, None] >= all_pos[None, :])[None], placed, masked_value)


def bias_grad(score_sum, tables, layout):
    own_block, own_pos, all_pos, perm = layout
    hot_rev = tables[2]
    head_count = score_sum.shape[0]
    seq_len = all_pos.shape[0]
    num_blocks = perm.shape[0]
    ordered = jnp.einsum(
        "hjci,cb->hjbi",
        score_sum.reshape(head_count, BLK, num_blocks, BLK),
        perm,
        precision=HIGHEST,
    )
    ordered = ordered.reshape(head_count, BLK, seq_len)[:, ::-1, :]
    sums = skew_sum(ordered)
    hot_window = lax.dynamic_slice_in_dim(hot_rev, window_start(layout), seq_len + BLK - 1, 0)
    return jnp.dot(sums, hot_window, precision=HIGHEST)


def seq_forward(query_rows, key_rows, value_rows, pos_bias):
    scores = (
        jnp.einsum("qhd,khd->hqk", query_rows, key_rows, preferred_element_type=jnp.float32) * 0.125
        + pos_bias
    )
    row_top = jnp.max(scores, axis=-1, keepdims=True)
    expo_rows = jnp.exp(scores - row_top)
    row_total = jnp.sum(expo_rows, axis=-1, keepdims=True)
    attn_probs = expo_rows / row_total
    mixed = jnp.einsum(
        "hqk,khd->qhd",
        attn_probs.astype(jnp.bfloat16),
        value_rows,
        preferred_element_type=jnp.float32,
    )
    return (mixed, (row_top + jnp.log(row_total))[..., 0])


def seq_backward(query_rows, key_rows, value_rows, grad_rows, pos_bias, log_total, row_delta):
    scores = (
        jnp.einsum("qhd,khd->hqk", query_rows, key_rows, preferred_element_type=jnp.float32) * 0.125
        + pos_bias
    )
    attn_probs = jnp.exp(scores - log_total[:, :, None])
    grad_probs = jnp.einsum(
        "qhd,khd->hqk", grad_rows, value_rows, preferred_element_type=jnp.float32
    )
    row_delta = jnp.sum(attn_probs * grad_probs, axis=-1)
    grad_scores = (attn_probs * (grad_probs - row_delta[:, :, None])).astype(jnp.bfloat16)
    return (attn_probs, grad_scores, row_delta)


def attention_forward(normed_low, gathered, bias_own):
    query_w, key_w, value_w, output_w = gathered
    feat_width = query_w.shape[1]
    head_count = feat_width // HS
    queries = jnp.dot(normed_low, query_w, preferred_element_type=jnp.float32).astype(jnp.bfloat16)
    keys_own = jnp.dot(normed_low, key_w, preferred_element_type=jnp.float32).astype(jnp.bfloat16)
    values_own = jnp.dot(normed_low, value_w, preferred_element_type=jnp.float32).astype(
        jnp.bfloat16
    )
    keys_all, values_all = (
        lax.all_gather(keys_own.reshape(1, SEQS, BLK, feat_width), "ctx", axis=0, tiled=True),
        lax.all_gather(values_own.reshape(1, SEQS, BLK, feat_width), "ctx", axis=0, tiled=True),
    )
    num_blocks = keys_all.shape[0]
    query_seq = queries.reshape(SEQS, BLK, head_count, HS)

    def one_seq(seq_index):
        key_seq = lax.dynamic_index_in_dim(keys_all, seq_index, 1, keepdims=False).reshape(
            num_blocks * BLK, head_count, HS
        )
        value_seq = lax.dynamic_index_in_dim(values_all, seq_index, 1, keepdims=False).reshape(
            num_blocks * BLK, head_count, HS
        )
        return seq_forward(query_seq[seq_index], key_seq, value_seq, bias_own)

    mixed, log_total = lax.map(one_seq, jnp.arange(SEQS))
    mixed_low = mixed.reshape(SEQS * BLK, feat_width).astype(jnp.bfloat16)
    branch = half_total(
        jnp.einsum("te,de->td", mixed_low, output_w, preferred_element_type=jnp.float32)
    )
    return (branch, (queries, keys_own, values_own, keys_all, values_all, mixed_low, log_total))


def attention_backward(grad_branch, normed_low, gathered, kept_fwd, tables, layout, bias_own):
    query_w, key_w, value_w, output_w = gathered
    queries, keys_own, values_own, keys_all, values_all, mixed_low, log_total = kept_fwd
    feat_width = query_w.shape[1]
    head_count = feat_width // HS
    num_blocks = keys_all.shape[0]
    grad_low = grad_branch.astype(jnp.bfloat16)
    output_grad = jnp.einsum("td,te->de", grad_low, mixed_low, preferred_element_type=jnp.float32)
    grad_mixed = jnp.einsum(
        "td,de->te", grad_low, output_w, preferred_element_type=jnp.float32
    ).astype(jnp.bfloat16)
    query_seq = queries.reshape(SEQS, BLK, head_count, HS)
    grad_seq = grad_mixed.reshape(SEQS, BLK, head_count, HS)

    def one_seq(score_sum, seq_index):
        key_seq = lax.dynamic_index_in_dim(keys_all, seq_index, 1, keepdims=False).reshape(
            num_blocks * BLK, head_count, HS
        )
        value_seq = lax.dynamic_index_in_dim(values_all, seq_index, 1, keepdims=False).reshape(
            num_blocks * BLK, head_count, HS
        )
        attn_probs, grad_scores, row_delta = seq_backward(
            query_seq[seq_index],
            key_seq,
            value_seq,
            grad_seq[seq_index],
            bias_own,
            log_total[seq_index],
            None,
        )
        grad_query = (
            jnp.einsum("hqk,khd->qhd", grad_scores, key_seq, preferred_element_type=jnp.float32)
            * 0.125
        )
        new_sum = score_sum + grad_scores.astype(jnp.float32)
        grad_key = (
            jnp.einsum(
                "hqk,qhd->khd",
                grad_scores,
                query_seq[seq_index],
                preferred_element_type=jnp.float32,
            )
            * 0.125
        )
        grad_value = jnp.einsum(
            "hqk,qhd->khd",
            attn_probs.astype(jnp.bfloat16),
            grad_seq[seq_index],
            preferred_element_type=jnp.float32,
        )
        return (
            new_sum,
            (
                grad_query.reshape(BLK, feat_width),
                grad_key.reshape(num_blocks, BLK, feat_width),
                grad_value.reshape(num_blocks, BLK, feat_width),
            ),
        )

    score_sum, stacked = lax.scan(one_seq, jnp.zeros(bias_own.shape, jnp.float32), jnp.arange(SEQS))
    grad_queries = stacked[0].reshape(SEQS * BLK, feat_width).astype(jnp.bfloat16)
    key_part, value_part = (
        lax.psum_scatter(stacked[1], "ctx", scatter_dimension=1, tiled=True),
        lax.psum_scatter(stacked[2], "ctx", scatter_dimension=1, tiled=True),
    )
    grad_keys = key_part.reshape(SEQS * BLK, feat_width).astype(jnp.bfloat16)
    grad_values = value_part.reshape(SEQS * BLK, feat_width).astype(jnp.bfloat16)
    rel_grad = bias_grad(score_sum, tables, layout)
    query_grad = jnp.einsum(
        "td,te->de", normed_low, grad_queries, preferred_element_type=jnp.float32
    )
    key_grad = jnp.einsum("td,te->de", normed_low, grad_keys, preferred_element_type=jnp.float32)
    value_grad = jnp.einsum(
        "td,te->de", normed_low, grad_values, preferred_element_type=jnp.float32
    )
    grad_partial = jnp.einsum(
        "te,de->td", grad_queries, query_w, preferred_element_type=jnp.float32
    )
    grad_partial = grad_partial + jnp.einsum(
        "te,de->td", grad_keys, key_w, preferred_element_type=jnp.float32
    )
    grad_partial = grad_partial + jnp.einsum(
        "te,de->td", grad_values, value_w, preferred_element_type=jnp.float32
    )
    return (half_total(grad_partial), (query_grad, key_grad, value_grad, output_grad), rel_grad)


def expert_block(normed, routes, router, expert_up, expert_down, grad_out):
    normed_low = normed.astype(jnp.bfloat16)
    tok_rows, top_count = routes.shape
    num_experts = router.shape[1]
    local_experts = expert_up.shape[0]
    model_width = normed.shape[1]
    capacity = 2 * tok_rows * top_count // num_experts
    flat_routes = routes.reshape(-1)
    one_hot = (flat_routes[:, None] == jnp.arange(num_experts, dtype=jnp.int32)[None, :]).astype(
        jnp.int32
    )
    slot_rank = jnp.sum((jnp.cumsum(one_hot, axis=0) - one_hot) * one_hot, axis=1)
    slot_place = flat_routes * capacity + slot_rank
    pick_mask = slot_place[:, None] == jnp.arange(num_experts * capacity, dtype=jnp.int32)[None, :]
    pick_low = pick_mask.astype(jnp.bfloat16)
    pick_full = pick_mask.astype(jnp.float32)
    repeated = jnp.repeat(normed_low, top_count, axis=0)
    outgoing = jnp.einsum(
        "ip,id->pd", pick_low, repeated, preferred_element_type=jnp.float32
    ).astype(jnp.bfloat16)
    arrived = lax.all_to_all(
        outgoing.reshape(num_experts, capacity, model_width),
        "ctx",
        split_axis=0,
        concat_axis=0,
        tiled=True,
    )
    arrived = arrived.reshape(-1, local_experts, capacity, model_width)
    pre_act = jnp.einsum("necd,edf->necf", arrived, expert_up, preferred_element_type=jnp.float32)
    hidden = gelu_fn(pre_act).astype(jnp.bfloat16)
    partial_value = jnp.einsum(
        "necf,efd->necd", hidden, expert_down, preferred_element_type=jnp.float32
    ).astype(jnp.bfloat16)
    returned = lax.all_to_all(
        partial_value.reshape(num_experts, capacity, model_width),
        "ctx",
        split_axis=0,
        concat_axis=0,
        tiled=True,
    )
    per_choice = half_total(
        jnp.einsum(
            "ip,pd->id",
            pick_low,
            returned.reshape(-1, model_width),
            preferred_element_type=jnp.float32,
        )
    )
    per_choice = per_choice.reshape(tok_rows, top_count, model_width)
    logits = jnp.dot(normed, router, precision=HIGHEST)
    route_hot = (
        routes[..., None] == jnp.arange(num_experts, dtype=jnp.int32)[None, None, :]
    ).astype(jnp.float32)
    chosen_logits = jnp.sum(logits[:, None, :] * route_hot, axis=-1)
    gate_probs = jax.nn.softmax(chosen_logits, axis=-1)
    mixture = jnp.sum(gate_probs[..., None] * per_choice, axis=1)
    grad_gate = jnp.sum(grad_out[:, None, :] * per_choice, axis=-1)
    grad_chosen = gate_probs * (grad_gate - jnp.sum(gate_probs * grad_gate, axis=-1, keepdims=True))
    grad_logits = jnp.sum(grad_chosen[..., None] * route_hot, axis=1)
    router_grad = jnp.dot(normed.T, grad_logits, precision=HIGHEST)
    grad_from_router = jnp.dot(grad_logits, router.T, precision=HIGHEST)
    grad_choice = (
        (gate_probs[..., None] * grad_out[:, None, :]).reshape(-1, model_width).astype(jnp.bfloat16)
    )
    grad_send = jnp.einsum(
        "ip,id->pd", pick_low, grad_choice, preferred_element_type=jnp.float32
    ).astype(jnp.bfloat16)
    grad_arrived = lax.all_to_all(
        grad_send.reshape(num_experts, capacity, model_width),
        "ctx",
        split_axis=0,
        concat_axis=0,
        tiled=True,
    )
    grad_arrived = grad_arrived.reshape(-1, local_experts, capacity, model_width)
    grad_hidden = jnp.einsum(
        "necd,efd->necf", grad_arrived, expert_down, preferred_element_type=jnp.float32
    )
    _, gelu_pull = jax.vjp(gelu_fn, pre_act)
    grad_pre = gelu_pull(grad_hidden)[0].astype(jnp.bfloat16)
    down_grad = jnp.einsum(
        "necf,necd->efd", hidden, grad_arrived, preferred_element_type=jnp.float32
    )
    up_grad = jnp.einsum("necd,necf->edf", arrived, grad_pre, preferred_element_type=jnp.float32)
    grad_inputs = jnp.einsum(
        "necf,edf->necd", grad_pre, expert_up, preferred_element_type=jnp.float32
    )
    grad_back = lax.all_to_all(
        grad_inputs.reshape(num_experts, capacity, model_width).astype(jnp.bfloat16),
        "ctx",
        split_axis=0,
        concat_axis=0,
        tiled=True,
    ).astype(jnp.float32)
    grad_rows = jnp.dot(pick_full, grad_back.reshape(-1, model_width), precision=HIGHEST)
    grad_normed = (
        half_total(jnp.sum(grad_rows.reshape(tok_rows, top_count, model_width), axis=1))
        + grad_from_router
    )
    return (mixture, grad_normed, router_grad, up_grad, down_grad)


def local(
    tokens,
    cotangent,
    routes,
    buckets,
    block_order,
    attend_gain1,
    rel_bias1,
    query_proj1,
    key_proj1,
    value_proj1,
    output_proj1,
    dense_gain1,
    dense_up1,
    dense_down1,
    attend_gain2,
    rel_bias2,
    query_proj2,
    key_proj2,
    value_proj2,
    output_proj2,
    expert_gain2,
    router,
    expert_up,
    expert_down,
):
    block_count = lax.axis_size("ctx")
    own_block = jnp.sum(
        block_order
        * (jnp.arange(block_count, dtype=jnp.int32) == lax.axis_index("ctx")).astype(jnp.int32)
    )
    offsets = jnp.arange(BLK, dtype=jnp.int32)
    own_pos = own_block * BLK + offsets
    all_pos = (block_order[:, None] * BLK + offsets[None, :]).reshape(-1)
    perm = (block_order[:, None] == jnp.arange(block_count, dtype=jnp.int32)[None, :]).astype(
        jnp.float32
    )
    layout = (own_block, own_pos, all_pos, perm)
    tables_one = bias_tables(rel_bias1, buckets)
    tables_two = bias_tables(rel_bias2, buckets)
    bias_one = query_bias(tables_one, layout)
    bias_two = query_bias(tables_two, layout)
    residual = tokens.astype(jnp.float32)
    normed_a1, inv_a1 = rms_norm(residual, attend_gain1)
    low_a1 = normed_a1.astype(jnp.bfloat16)
    gathered_one = gather_attention((query_proj1, key_proj1, value_proj1, output_proj1))
    branch_a1, kept_a1 = attention_forward(low_a1, gathered_one, bias_one)
    after_attn1 = residual + branch_a1
    normed_d1, inv_d1 = rms_norm(after_attn1, dense_gain1)
    low_d1 = normed_d1.astype(jnp.bfloat16)
    up_full, down_full = (
        lax.all_gather(dense_up1, "ctx", axis=0, tiled=True),
        lax.all_gather(dense_down1, "ctx", axis=0, tiled=True),
    )
    pre_d1 = jnp.dot(low_d1, up_full, preferred_element_type=jnp.float32)
    hidden_d1 = gelu_fn(pre_d1).astype(jnp.bfloat16)
    after_dense1 = after_attn1 + half_total(
        jnp.einsum("tf,df->td", hidden_d1, down_full, preferred_element_type=jnp.float32)
    )
    normed_a2, inv_a2 = rms_norm(after_dense1, attend_gain2)
    low_a2 = normed_a2.astype(jnp.bfloat16)
    gathered_two = gather_attention((query_proj2, key_proj2, value_proj2, output_proj2))
    branch_a2, kept_a2 = attention_forward(low_a2, gathered_two, bias_two)
    after_attn2 = after_dense1 + branch_a2
    normed_e2, inv_e2 = rms_norm(after_attn2, expert_gain2)
    grad_out = cotangent.astype(jnp.float32)
    mixture, grad_normed_e2, router_grad, up_grad, down_grad = expert_block(
        normed_e2, routes, router, expert_up, expert_down, grad_out
    )
    result = (after_attn2 + mixture).astype(jnp.bfloat16)
    grad_part, gain_e2 = norm_back(after_attn2, inv_e2, expert_gain2, grad_normed_e2)
    grad_residual = grad_out + grad_part
    grad_normed_a2, two_grads, rel_two = attention_backward(
        grad_residual, low_a2, gathered_two, kept_a2, tables_two, layout, bias_two
    )
    query_two, key_two, value_two, output_two = scatter_attention(two_grads)
    grad_part, gain_a2 = norm_back(after_dense1, inv_a2, attend_gain2, grad_normed_a2)
    grad_residual = grad_residual + grad_part
    grad_low = grad_residual.astype(jnp.bfloat16)
    down_part = jnp.einsum("td,tf->df", grad_low, hidden_d1, preferred_element_type=jnp.float32)
    grad_hidden = jnp.einsum("td,df->tf", grad_low, down_full, preferred_element_type=jnp.float32)
    _, gelu_pull = jax.vjp(gelu_fn, pre_d1)
    grad_pre = gelu_pull(grad_hidden)[0].astype(jnp.bfloat16)
    up_part = jnp.einsum("td,tf->df", low_d1, grad_pre, preferred_element_type=jnp.float32)
    grad_normed_d1 = half_total(
        jnp.einsum("tf,df->td", grad_pre, up_full, preferred_element_type=jnp.float32)
    )
    dense_up_grad, dense_down_grad = sent_together(
        (up_part.astype(jnp.bfloat16), down_part.astype(jnp.bfloat16)), "ctx", 0, 1
    )
    grad_part, gain_d1 = norm_back(after_attn1, inv_d1, dense_gain1, grad_normed_d1)
    grad_residual = grad_residual + grad_part
    grad_normed_a1, one_grads, rel_one = attention_backward(
        grad_residual, low_a1, gathered_one, kept_a1, tables_one, layout, bias_one
    )
    query_one, key_one, value_one, output_one = scatter_attention(one_grads)
    grad_part, gain_a1 = norm_back(residual, inv_a1, attend_gain1, grad_normed_a1)
    grad_tokens = grad_residual + grad_part
    summed = lax.psum((gain_a1, gain_d1, gain_a2, gain_e2, rel_one, rel_two, router_grad), "ctx")
    return (
        result,
        grad_tokens,
        summed[0],
        summed[4],
        query_one,
        key_one,
        value_one,
        output_one,
        summed[1],
        dense_up_grad,
        dense_down_grad,
        summed[2],
        summed[5],
        query_two,
        key_two,
        value_two,
        output_two,
        summed[3],
        summed[6],
        up_grad,
        down_grad,
    )


def solution(mesh):
    placed = (
        P("ctx", None),
        P("ctx", None),
        P("ctx", None),
        P(),
        P(),
        P(),
        P("wa", None),
        P("ctx", "wa"),
        P("ctx", "wa"),
        P("ctx", "wa"),
        P("ctx", "wa"),
        P(),
        P("ctx", "wa"),
        P("ctx", "wa"),
        P(),
        P("wa", None),
        P("ctx", "wa"),
        P("ctx", "wa"),
        P("ctx", "wa"),
        P("ctx", "wa"),
        P(),
        P(),
        P("ctx", None, "wa"),
        P("ctx", "wa", None),
    )
    return jax.shard_map(
        local,
        mesh=mesh,
        in_specs=placed,
        out_specs=(
            P("ctx", None),
            P("ctx", None),
            P(),
            P("wa", None),
            P("ctx", "wa"),
            P("ctx", "wa"),
            P("ctx", "wa"),
            P("ctx", "wa"),
            P(),
            P("ctx", "wa"),
            P("ctx", "wa"),
            P(),
            P("wa", None),
            P("ctx", "wa"),
            P("ctx", "wa"),
            P("ctx", "wa"),
            P("ctx", "wa"),
            P(),
            P(),
            P("ctx", None, "wa"),
            P("ctx", "wa", None),
        ),
        check_vma=False,
    )
```

profile of v0, /device:TPU:0, one launch (start us, length us, event | category | flops | bytes accessed | tf_op | source)
XLA Modules:
  0.0 2246.1 jit_solution(11733342362941458151)
XLA Ops:
  7.3 46.0 %all_gather.42 = bf16[768,384]{1,0:T(8,128)(2,1)S(1)} all-gather(bf16[48,384]{1,0:T(8,128)(2,1)} %param.41), channel_id=1, replica_groups=mesh['ctx'=16,'wa'=2] {'ctx'}, dimensions={0}, use_global_device_ids=true | all-gather | bytes 626688 | tf_op jit(solution)/shard_map/all_gather | solution.py:62
  56.9 41.5 %all_gather.45 = bf16[768,384]{1,0:T(8,128)(2,1)S(1)} all-gather(bf16[48,384]{1,0:T(8,128)(2,1)S(1)} %copy-done.91), channel_id=1, replica_groups=mesh['ctx'=16,'wa'=2] {'ctx'}, dimensions={0}, use_global_device_ids=true | all-gather | bytes 626688 | tf_op jit(solution)/shard_map/all_gather | solution.py:61
  100.4 44.0 %all_gather.44 = bf16[768,384]{1,0:T(8,128)(2,1)S(1)} all-gather(bf16[48,384]{1,0:T(8,128)(2,1)S(1)} %copy-done.92), channel_id=1, replica_groups=mesh['ctx'=16,'wa'=2] {'ctx'}, dimensions={0}, use_global_device_ids=true | all-gather | bytes 626688 | tf_op jit(solution)/shard_map/all_gather | solution.py:60
  167.6 5.4 rev.25
  199.4 5.5 rev.23
  216.4 41.2 %all_gather.47 = bf16[768,384]{1,0:T(8,128)(2,1)} all-gather(bf16[48,384]{1,0:T(8,128)(2,1)S(1)} %copy-done.93), channel_id=1, replica_groups=mesh['ctx'=16,'wa'=2] {'ctx'}, dimensions={0}, use_global_device_ids=true | all-gather | bytes 626688 | tf_op jit(solution)/shard_map/all_gather | solution.py:63
  261.9 7.8 copy.193
  269.7 7.9 copy.195
  278.9 71.3 %while.58 = (s32[]{:T(128)}, bf16[4,64,6,64]{1,3,2,0:T(8,128)(2,1)}, f32[4,6,64]{2,1,0:T(8,128)S(1)}, s32[4]{0:T(128)}, bf16[16,4,64,384]{2,0,3,1:T(8,128)(2,1)}...) while((s32[]{:T(128)}, ...), condition=%wide.region_5.6_spmd, body=%wide.region_2.5_spmd.sunk | while | flops 103808640 | bytes 19194632 | solution.py:206
  356.6 15.1 all-reduce.15.cloned.1.call-done
  372.9 65.3 %all-gather.11.cloned.1.call-done = bf16[768,1536]{1,0:T(8,128)(2,1)} async-done(((bf16[48,1536]{1,0:T(8,128)(2,1)}), bf16[768,1536]{1,0:T(8,128)(2,1)}) %all-gather.11.cloned.1.call-update) | async-done | bytes 2359312 | tf_op jit(solution)/shard_map/all_gather | solution.py:454
  442.1 60.3 %all-gather.13.cloned.1.call-done = bf16[768,1536]{1,0:T(8,128)(2,1)} async-done(((bf16[48,1536]{1,0:T(8,128)(2,1)}), bf16[768,1536]{1,0:T(8,128)(2,1)}) %all-gather.13.cloned.1.call-update) | async-done | bytes 2359312 | tf_op jit(solution)/shard_map/all_gather | solution.py:455
  506.5 44.5 %all_gather.50 = bf16[768,384]{1,0:T(8,128)(2,1)} all-gather(bf16[48,384]{1,0:T(8,128)(2,1)S(1)} %copy-done.94), channel_id=1, replica_groups=mesh['ctx'=16,'wa'=2] {'ctx'}, dimensions={0}, use_global_device_ids=true | all-gather | bytes 626688 | tf_op jit(solution)/shard_map/all_gather | solution.py:62
  553.7 41.5 %all_gather.53 = bf16[768,384]{1,0:T(8,128)(2,1)S(1)} all-gather(bf16[48,384]{1,0:T(8,128)(2,1)} %param.49), channel_id=1, replica_groups=mesh['ctx'=16,'wa'=2] {'ctx'}, dimensions={0}, use_global_device_ids=true | all-gather | bytes 626688 | tf_op jit(solution)/shard_map/all_gather | solution.py:61
  599.2 45.2 %all_gather.52 = bf16[768,384]{1,0:T(8,128)(2,1)S(1)} all-gather(bf16[48,384]{1,0:T(8,128)(2,1)} %param.48), channel_id=1, replica_groups=mesh['ctx'=16,'wa'=2] {'ctx'}, dimensions={0}, use_global_device_ids=true | all-gather | bytes 626688 | tf_op jit(solution)/shard_map/all_gather | solution.py:60
  644.4 44.0 %all_gather.55 = bf16[768,384]{1,0:T(8,128)(2,1)} all-gather(bf16[48,384]{1,0:T(8,128)(2,1)} %param.51), channel_id=1, replica_groups=mesh['ctx'=16,'wa'=2] {'ctx'}, dimensions={0}, use_global_device_ids=true | all-gather | bytes 626688 | tf_op jit(solution)/shard_map/all_gather | solution.py:63
  691.1 7.9 copy.199
  699.0 7.8 copy.201
  708.1 71.0 %while.59 = (s32[]{:T(128)}, bf16[4,64,6,64]{1,3,2,0:T(8,128)(2,1)}, f32[4,6,64]{2,1,0:T(8,128)S(1)}, s32[4]{0:T(128)}, bf16[16,4,64,384]{2,0,3,1:T(8,128)(2,1)}...) while((s32[]{:T(128)}, ...), condition=%wide.region_13.14_spmd, body=%wide.region_10.13_spmd.sunk | while | flops 103808640 | bytes 19194632 | solution.py:206
  787.2 13.8 all-reduce.19.cloned.1.call-done
  810.3 7.2 all-to-all-start
  835.0 16.9 all-to-all-done
  851.8 8.2 all-to-all-start.2
  867.4 4.8 fusion.72
  872.2 21.7 all-to-all-done.2
  893.9 7.3 all-to-all-start.1
  901.2 8.1 fusion.51
  914.9 20.0 all-to-all-done.1
  934.9 7.3 all-to-all-start.3
  946.0 29.7 %all-to-all-done.3 = bf16[16,64,768]{2,1,0:T(8,128)(2,1)S(1)} async-done(((bf16[16,64,768]{2,1,0:T(8,128)(2,1)}), bf16[16,64,768]{2,1,0:T(8,128)(2,1)S(1)}, u32[]{:S(2)}, u32[]{:S(2)}) %all-to-all-start.3) | async-done | bytes 1572896 | tf_op jit(solution)/shard_map/all_to_all | solution.py:388
  980.4 21.7 all-reduce.27.cloned.1.call-done
  1023.5 147.4 %while.60 = (s32[]{:T(128)}, f32[6,64,1024]{2,1,0:T(8,128)}, bf16[4,64,384]{2,1,0:T(8,128)(2,1)}, f32[4,16,64,384]{3,2,0,1:T(8,128)}, f32[4,16,64,384]{3,2,0,1:T...) while((s32[]{:T(128)}, f32[6,64,1024]{2,1,0:T(8,128)}, ...), condition=%wide.region_32.33_spmd.clone, body=%wide.region_30.32_spmd.clone.sunk | while | flops 256818816 | bytes 63564100 | solution.py:273
  1172.5 146.1 %reduce-scatter.5.cloned.1.call-done = f32[4,1,64,384]{3,2,0,1:T(8,128)} async-done(((f32[4,16,64,384]{3,2,0,1:T(8,128)}), f32[4,1,64,384]{3,2,0,1:T(8,128)}) %reduce-scatter.5.cloned.1.call-update) | async-done | bytes 393232 | tf_op jit(solution)/shard_map/reduce_scatter | solution.py:276
  1320.9 147.5 %reduce-scatter.7.cloned.1.call-done = f32[4,1,64,384]{3,2,0,1:T(8,128)} async-done(((f32[4,16,64,384]{3,2,0,1:T(8,128)}), f32[4,1,64,384]{3,2,0,1:T(8,128)}) %reduce-scatter.7.cloned.1.call-update) | async-done | bytes 393232 | tf_op jit(solution)/shard_map/reduce_scatter | solution.py:277
  1472.6 17.8 all-reduce.21.cloned.1.call-done
  1497.9 19.3 all-reduce.23.cloned.1.call-done
  1529.7 147.4 %while.61 = (s32[]{:T(128)}, f32[6,64,1024]{2,1,0:T(8,128)}, bf16[4,64,384]{2,1,0:T(8,128)(2,1)}, f32[4,16,64,384]{3,2,0,1:T(8,128)}, f32[4,16,64,384]{3,2,0,1:T...) while((s32[]{:T(128)}, f32[6,64,1024]{2,1,0:T(8,128)}, ...), condition=%wide.region_41.42_spmd.clone, body=%wide.region_39.41_spmd.clone.sunk | while | flops 256818816 | bytes 63561540 | solution.py:273
  1686.1 7.1 all-to-all-start.6
  1699.2 65.9 %all-to-all-done.6 = bf16[16,48,1536]{2,1,0:T(8,128)(2,1)S(1)} async-done(((bf16[16,48,1536]{2,1,0:T(8,128)(2,1)}), bf16[16,48,1536]{2,1,0:T(8,128)(2,1)S(1)}, u32[]{:S(2)}, u32[]{:S(2)}) %all-to-all-start.6) | async-done | bytes 2359328 | tf_op jit(solution)/shard_map/all_to_all | solution.py:23
  1766.5 15.2 all-to-all-start.5
  1782.0 5.2 rev.27
  1787.3 9.3 convolution_bitcast_fusion.4
  1798.1 115.4 %reduce-scatter.9.cloned.1.call-done = f32[4,1,64,384]{3,2,0,1:T(8,128)} async-done(((f32[4,16,64,384]{3,2,0,1:T(8,128)}), f32[4,1,64,384]{3,2,0,1:T(8,128)}) %reduce-scatter.9.cloned.1.call-update) | async-done | bytes 393232 | tf_op jit(solution)/shard_map/reduce_scatter | solution.py:276
  1914.5 150.0 %reduce-scatter.11.cloned.1.call-done = f32[4,1,64,384]{3,2,0,1:T(8,128)} async-done(((f32[4,16,64,384]{3,2,0,1:T(8,128)}), f32[4,1,64,384]{3,2,0,1:T(8,128)}) %reduce-scatter.11.cloned.1.call-update) | async-done | bytes 393232 | tf_op jit(solution)/shard_map/reduce_scatter | solution.py:277
  2069.4 4.8 all-to-all-start.4
  2074.4 7.3 convolution_bitcast_fusion.5
  2135.2 19.1 all-reduce.25.cloned.1.call-done
  2155.6 78.5 %all-reduce.5 = (f32[768]{0:T(1024)}, f32[6,32]{1,0:T(8,128)}, f32[768]{0:T(1024)}, f32[768]{0:T(1024)}, f32[6,32]{1,0:T(8,128)}, /*index=5*/f32[768]{0:T(1024)}, f32[768,16]{0,1:T(8,128)}) all-reduce(f32[768]{0:T(1024)S(1)} %get-tuple-element.533, f32[6,32]{1,0:T(8,128)S(1)} %fusion.128, ...), channel_id=1, replica_groups=mesh['ctx'=16,'wa'=2] {'ctx'}, use_global_device_ids=true, to_apply=%region_47.48 | all-reduce | flops 15744 | bytes 125952 | tf_op jit(solution)/shard_map/psum | solution.py:501
  (758 shorter events, 691.1 us)
Async XLA Ops:
  7.2 860.2 %copy-start = (bf16[1,1536,768]{2,1,0:T(8,128)(2,1)S(1)}, bf16[1,1536,768]{2,1,0:T(8,128)(2,1)}, u32[]{:S(2)}) copy-start(bf16[1,1536,768]{2,1,0:T(8,128)(2,1)} %param.55) | copy-start | bytes 7077892
  7.2 49.7 %copy-start.91 = (bf16[48,384]{1,0:T(8,128)(2,1)S(1)}, bf16[48,384]{1,0:T(8,128)(2,1)}, u32[]{:S(2)}) copy-start(bf16[48,384]{1,0:T(8,128)(2,1)} %param.40) | copy-start | bytes 110596
  7.2 92.0 %copy-start.10 = (bf16[256,768]{1,0:T(8,128)(2,1)S(1)}, bf16[256,768]{1,0:T(8,128)(2,1)}, u32[]{:S(2)}) copy-start(bf16[256,768]{1,0:T(8,128)(2,1)} %param.32) | copy-start | bytes 1179652
  7.2 92.0 %copy-start.101 = (f32[768]{0:T(1024)S(1)}, f32[768]{0:T(1024)}, u32[]{:S(2)}) copy-start(f32[768]{0:T(1024)} %param.37) | copy-start | bytes 9220
  7.2 254.6 %all-gather.7.cloned.1.call-start = ((), (), s32[]{:S(2)}) async-start(), calls=%async_computation.11 | async-start | bytes 3342336 | tf_op jit(solution)/shard_map/all_gather | solution.py:192
  53.3 47.0 %copy-start.47 = (bf16[768,384]{1,0:T(8,128)(2,1)}, bf16[768,384]{1,0:T(8,128)(2,1)S(1)}, u32[]{:S(2)}) copy-start(bf16[768,384]{1,0:T(8,128)(2,1)S(1)} %all_gather.42) | copy-start | bytes 1769476
  54.7 89.8 %copy-start.111 = (f32[256]{0:T(256)}, f32[256]{0:T(256)S(1)}, u32[]{:S(2)}) copy-start(f32[256]{0:T(256)S(1)} %add_rsqrt_fusion.3) | copy-start | bytes 3076
  56.8 212.9 %all-gather.9.cloned.1.call-start = ((), (), s32[]{:S(2)}) async-start(), calls=%async_computation.12 | async-start | bytes 3342336 | tf_op jit(solution)/shard_map/all_gather | solution.py:191
  100.3 271.4 %all-reduce.15.cloned.1.call-start = ((), (), s32[]{:S(2)}) async-start(), calls=%async_computation.13 | async-start | bytes 786432 | tf_op jit(solution)/shard_map/psum | solution.py:55
  352.9 85.4 %copy-start.81 = (f32[768]{0:T(1024)S(1)}, f32[768]{0:T(1024)}, u32[]{:S(2)}) copy-start(f32[768]{0:T(1024)} %param.43) | copy-start | bytes 9220
  354.2 87.9 %copy-start.53 = (bf16[256,384]{0,1:T(8,128)(2,1)}, bf16[256,384]{0,1:T(8,128)(2,1)S(1)}, u32[]{:S(2)}) copy-start(bf16[256,384]{0,1:T(8,128)(2,1)S(1)} %convert_element_type.267) | copy-start | bytes 589828
  355.4 82.9 %all-gather.11.cloned.1.call-start = ((), (), s32[]{:S(2)}) async-start(), calls=%async_computation.14 | async-start | bytes 2506752 | tf_op jit(solution)/shard_map/all_gather | solution.py:454
  356.0 146.5 %all-gather.13.cloned.1.call-start = ((), (), s32[]{:S(2)}) async-start(), calls=%async_computation.15 | async-start | bytes 2506752 | tf_op jit(solution)/shard_map/all_gather | solution.py:455
  356.6 194.4 %all-reduce.17.cloned.1.call-start = ((), (), s32[]{:S(2)}) async-start(), calls=%async_computation.16 | async-start | bytes 786432 | tf_op jit(solution)/shard_map/psum | solution.py:55
  372.9 69.2 %copy-start.87 = (f32[256]{0:T(256)}, f32[256]{0:T(256)S(1)}, u32[]{:S(2)}) copy-start(f32[256]{0:T(256)S(1)} %add_rsqrt_fusion.2) | copy-start | bytes 3076
  442.1 64.4 %copy-start.94 = (bf16[48,384]{1,0:T(8,128)(2,1)S(1)}, bf16[48,384]{1,0:T(8,128)(2,1)}, u32[]{:S(2)}) copy-start(bf16[48,384]{1,0:T(8,128)(2,1)} %param.50) | copy-start | bytes 110596
  506.4 46.0 %copy-start.89 = (f32[768]{0:T(1024)S(1)}, f32[768]{0:T(1024)}, u32[]{:S(2)}) copy-start(f32[768]{0:T(1024)} %param.46) | copy-start | bytes 9220
  506.4 184.7 %all-gather.15.cloned.1.call-start = ((), (), s32[]{:S(2)}) async-start(), calls=%async_computation.17 | async-start | bytes 3342336 | tf_op jit(solution)/shard_map/all_gather | solution.py:192
  552.6 135.9 %copy-start.18 = (bf16[256,768]{1,0:T(8,128)(2,1)}, bf16[256,768]{1,0:T(8,128)(2,1)S(1)}, u32[]{:S(2)}) copy-start(bf16[256,768]{1,0:T(8,128)(2,1)S(1)} %multiply_convert_fusion.5) | copy-start | bytes 1179652
  552.6 43.8 %copy-start.97 = (s32[256,2]{0,1:T(2,128)S(1)}, s32[256,2]{0,1:T(2,128)}, u32[]{:S(2)}) copy-start(s32[256,2]{0,1:T(2,128)} %param.34) | copy-start | bytes 6148
  553.7 145.3 %all-gather.17.cloned.1.call-start = ((), (), s32[]{:S(2)}) async-start(), calls=%async_computation.18 | async-start | bytes 3342336 | tf_op jit(solution)/shard_map/all_gather | solution.py:191
  596.3 204.8 %all-reduce.19.cloned.1.call-start = ((), (), s32[]{:S(2)}) async-start(), calls=%async_computation.19 | async-start | bytes 786432 | tf_op jit(solution)/shard_map/psum | solution.py:55
  644.4 46.6 %copy-start.33 = (bf16[768,384]{1,0:T(8,128)(2,1)}, bf16[768,384]{1,0:T(8,128)(2,1)S(1)}, u32[]{:S(2)}) copy-start(bf16[768,384]{1,0:T(8,128)(2,1)S(1)} %all_gather.52) | copy-start | bytes 1769476
  802.5 210.0 %copy-start.12 = (f32[256,768]{1,0:T(8,128)}, f32[256,768]{1,0:T(8,128)S(1)}, u32[]{:S(2)}) copy-start(f32[256,768]{1,0:T(8,128)S(1)} %get-tuple-element.629) | copy-start | bytes 2359300
  802.5 209.9 %copy-start.95 = (f32[256]{0:T(256)}, f32[256]{0:T(256)S(1)}, u32[]{:S(2)}) copy-start(f32[256]{0:T(256)S(1)} %add_rsqrt_fusion) | copy-start | bytes 3076
  810.3 41.5 %all-to-all-start = ((bf16[16,64,768]{2,1,0:T(8,128)(2,1)}), bf16[16,64,768]{2,1,0:T(8,128)(2,1)}, u32[]{:S(2)}, u32[]{:S(2)}) async-start(bf16[16,64,768]{2,1,0:T(8,128)(2,1)} %bitcast.441), calls=%async_computation | async-start | bytes 3145728 | tf_op jit(solution)/shard_map/all_to_all | solution.py:321
  851.8 42.0 %all-to-all-start.2 = ((bf16[16,64,768]{2,1,0:T(8,128)(2,1)}), bf16[16,64,768]{2,1,0:T(8,128)(2,1)}, u32[]{:S(2)}, u32[]{:S(2)}) async-start(bf16[16,64,768]{2,1,0:T(8,128)(2,1)} %bitcast.443), calls=%async_computation.2 | async-start | bytes 3145728 | tf_op jit(solution)/shard_map/all_to_all | solution.py:368
  893.9 41.0 %all-to-all-start.1 = ((bf16[16,64,768]{2,1,0:T(8,128)(2,1)}), bf16[16,64,768]{2,1,0:T(8,128)(2,1)}, u32[]{:S(2)}, u32[]{:S(2)}) async-start(bf16[16,64,768]{2,1,0:T(8,128)(2,1)} %fusion.72), calls=%async_computation.1 | async-start | bytes 3145728 | tf_op jit(solution)/shard_map/all_to_all | solution.py:334
  934.9 40.8 %all-to-all-start.3 = ((bf16[16,64,768]{2,1,0:T(8,128)(2,1)}), bf16[16,64,768]{2,1,0:T(8,128)(2,1)S(1)}, u32[]{:S(2)}, u32[]{:S(2)}) async-start(bf16[16,64,768]{2,1,0:T(8,128)(2,1)} %fusion.69), calls=%async_computation.3 | async-start | bytes 3145728 | tf_op jit(solution)/shard_map/all_to_all | solution.py:388
  942.2 59.9 %all-reduce.27.cloned.1.call-start = ((), (), s32[]{:S(2)}) async-start(), calls=%async_computation.27 | async-start | bytes 2359296 | tf_op jit(solution)/shard_map/psum | solution.py:55
  980.3 338.2 %reduce-scatter.5.cloned.1.call-start = ((), (), s32[]{:S(2)}) async-start(), calls=%async_computation.20 | async-start | bytes 6684672 | tf_op jit(solution)/shard_map/reduce_scatter | solution.py:276
  1170.9 297.5 %reduce-scatter.7.cloned.1.call-start = ((), (), s32[]{:S(2)}) async-start(), calls=%async_computation.21 | async-start | bytes 6684672 | tf_op jit(solution)/shard_map/reduce_scatter | solution.py:277
  1171.5 148.1 %copy-start.40 = (bf16[768,384]{1,0:T(8,128)(2,1)S(1)}, bf16[768,384]{1,0:T(8,128)(2,1)}, u32[]{:S(2)}) copy-start(bf16[768,384]{1,0:T(8,128)(2,1)} %copy-done.39) | copy-start | bytes 1769476
  1171.5 318.8 %all-reduce.21.cloned.1.call-start = ((), (), s32[]{:S(2)}) async-start(), calls=%async_computation.22 | async-start | bytes 786432 | tf_op jit(solution)/shard_map/psum | solution.py:55
  1319.6 149.9 %copy-start.57 = (bf16[4,1,64,384]{3,2,0,1:T(8,128)(2,1)}, bf16[4,1,64,384]{3,2,0,1:T(8,128)(2,1)S(1)}, u32[]{:S(2)}) copy-start(bf16[4,1,64,384]{3,2,0,1:T(8,128)(2,1)S(1)} %convert_element_type.302) | copy-start | bytes 589828
  1319.6 150.6 %copy-start.38 = (bf16[768,384]{1,0:T(8,128)(2,1)S(1)}, bf16[768,384]{1,0:T(8,128)(2,1)}, u32[]{:S(2)}) copy-start(bf16[768,384]{1,0:T(8,128)(2,1)} %all_gather.50) | copy-start | bytes 1769476
  1320.9 169.4 %copy-start.15 = (f32[256,768]{1,0:T(8,128)S(1)}, f32[256,768]{1,0:T(8,128)}, u32[]{:S(2)}) copy-start(f32[256,768]{1,0:T(8,128)} %copy-done.14) | copy-start | bytes 2359300
  1320.9 169.4 %copy-start.90 = (f32[768]{0:T(1024)S(1)}, f32[768]{0:T(1024)}, u32[]{:S(2)}) copy-start(f32[768]{0:T(1024)} %param.46) | copy-start | bytes 9220
  1320.9 169.4 %copy-start.108 = (f32[256]{0:T(256)S(1)}, f32[256]{0:T(256)}, u32[]{:S(2)}) copy-start(f32[256]{0:T(256)} %copy-done.107) | copy-start | bytes 3076
  1472.5 44.7 %all-reduce.23.cloned.1.call-start = ((), (), s32[]{:S(2)}) async-start(), calls=%async_computation.23 | async-start | bytes 786432 | tf_op jit(solution)/shard_map/psum | solution.py:55
  1497.5 416.0 %reduce-scatter.9.cloned.1.call-start = ((), (), s32[]{:S(2)}) async-start(), calls=%async_computation.24 | async-start | bytes 6684672 | tf_op jit(solution)/shard_map/reduce_scatter | solution.py:276
  1677.2 387.4 %reduce-scatter.11.cloned.1.call-start = ((), (), s32[]{:S(2)}) async-start(), calls=%async_computation.25 | async-start | bytes 6684672 | tf_op jit(solution)/shard_map/reduce_scatter | solution.py:277
  1686.1 78.9 %all-to-all-start.6 = ((bf16[16,48,1536]{2,1,0:T(8,128)(2,1)}), bf16[16,48,1536]{2,1,0:T(8,128)(2,1)S(1)}, u32[]{:S(2)}, u32[]{:S(2)}) async-start(bf16[16,48,1536]{2,1,0:T(8,128)(2,1)} %bitcast.432), calls=%async_computation.10 | async-start | bytes 4718592 | tf_op jit(solution)/shard_map/all_to_all | solution.py:23
  1766.5 302.9 %all-to-all-start.5 = ((bf16[16,48,3072]{2,1,0:T(8,128)(2,1)}), bf16[16,48,3072]{2,1,0:T(8,128)(2,1)}, u32[]{:S(2)}, u32[]{:S(2)}) async-start(bf16[16,48,3072]{2,1,0:T(8,128)(2,1)} %bitcast.429), calls=%async_computation.9 | async-start | bytes 9437184 | tf_op jit(solution)/shard_map/all_to_all | solution.py:23
  1914.5 152.4 %copy-start.73 = (bf16[4,1,64,384]{3,2,0,1:T(8,128)(2,1)}, bf16[4,1,64,384]{3,2,0,1:T(8,128)(2,1)S(1)}, u32[]{:S(2)}) copy-start(bf16[4,1,64,384]{3,2,0,1:T(8,128)(2,1)S(1)} %convert_element_type.316) | copy-start | bytes 589828
  2069.4 167.0 %all-to-all-start.4 = ((bf16[16,48,1536]{2,1,0:T(8,128)(2,1)}), bf16[16,48,1536]{2,1,0:T(8,128)(2,1)}, u32[]{:S(2)}, u32[]{:S(2)}) async-start(bf16[16,48,1536]{2,1,0:T(8,128)(2,1)} %bitcast.52), calls=%async_computation.8 | async-start | bytes 4718592 | tf_op jit(solution)/shard_map/all_to_all | solution.py:23
  2074.2 80.1 %all-reduce.25.cloned.1.call-start = ((), (), s32[]{:S(2)}) async-start(), calls=%async_computation.26 | async-start | bytes 786432 | tf_op jit(solution)/shard_map/psum | solution.py:55
  2134.3 99.8 %copy-start.27 = (f32[256,768]{1,0:T(8,128)S(1)}, f32[256,768]{1,0:T(8,128)}, u32[]{:S(2)}) copy-start(f32[256,768]{1,0:T(8,128)} %copy-done.25) | copy-start | bytes 2359300
  (134 other events, 719.0 us)
Sparse Core Ops, SparseCore 0:
  56.9 69.5 all-gather.6
  129.9 69.7 all-gather.8
  355.5 16.1 all-reduce.14
  374.7 63.4 all-gather.10
  441.3 61.0 all-gather.12
  506.5 17.2 all-reduce.16
  553.8 71.6 all-gather.14
  628.8 68.6 all-gather.16
  783.9 17.1 all-reduce.18
  980.5 21.5 all-reduce.26
  1171.0 147.4 reduce-scatter.4
  1323.7 144.7 reduce-scatter.6
  1472.7 17.6 all-reduce.20
  1497.6 19.6 all-reduce.22
  1677.3 236.1 reduce-scatter.8
  1918.6 145.9 reduce-scatter.10
  2134.5 19.7 all-reduce.24
where the time goes:
time: 2260 us; the launch traced here: 2250 us
  waiting for transfers between devices  947 us (42%)
  local copies, waits for them, and re-layouts  477 us (21%)
  blocking collectives  426 us (19%)
  matrix products  223 us (10%)
  other arithmetic  65.2 us (3%)
  starting transfers between devices  58.6 us (3%)
  loops' own time  32.4 us (1%)
    reduce_scatter x2, waiting for transfers between devices, attention_backward(): lax.psum_scatter(stacked[2], 'ctx', scatter_dimension=1, tiled=True)  298 us
    reduce_scatter x2, waiting for transfers between devices, attention_backward(): lax.psum_scatter(stacked[1], 'ctx', scatter_dimension=1, tiled=True)  261 us
    psum x7, waiting for transfers between devices, half_total(): lax.psum(partial_value.astype(jnp.bfloat16), 'wa').astype(jnp.float32)  107 us
    all_gather x2, blocking collectives, gather_attention(): lax.all_gather(weights[2], 'ctx', axis=0, tiled=True)  90.5 us
    all_gather x2, blocking collectives, gather_attention(): lax.all_gather(weights[0], 'ctx', axis=0, tiled=True)  89.3 us
    all_gather x2, blocking collectives, gather_attention(): lax.all_gather(weights[3], 'ctx', axis=0, tiled=True)  85.2 us
    all_gather x2, blocking collectives, gather_attention(): lax.all_gather(weights[1], 'ctx', axis=0, tiled=True)  83 us
    psum x1, blocking collectives, local(): lax.psum((gain_a1, gain_d1, gain_a2, gain_e2, rel_one, rel_two, router_gr...  78.5 us
  transfers between devices with their start and end apart: 24, of which 17 were waited for; matrix products, arithmetic and copies ran while one was open for 11% of the time, Pallas kernels for 0%

commit v1 on v0

v1 whole, which is shorter than its diff:
```python
import jax
import jax.numpy as jnp
from jax import lax
from jax.experimental import pallas as pl
from jax.experimental.pallas import tpu as pltpu
from jax.sharding import PartitionSpec as P

HS = 64
SEQS = 4
BLK = 64
TILE = 256
PER = TILE // BLK


HIGHEST = lax.Precision.HIGHEST
epsilon = 1e-06
masked_value = -1e30


def gelu_fn(values):
    return jax.nn.gelu(values, approximate=True)


def rms_norm(inputs, gain):
    inv_rms = lax.rsqrt(jnp.mean(inputs * inputs, axis=-1, keepdims=True) + epsilon)
    return (inputs * inv_rms * gain, inv_rms)


def norm_back(inputs, inv_rms, gain, grad_normed):
    weighted = grad_normed * gain
    gain_grad = jnp.sum(grad_normed * inputs * inv_rms, axis=0)
    grad_inputs = inv_rms * weighted - inputs * inv_rms * inv_rms * inv_rms * jnp.mean(
        weighted * inputs, axis=-1, keepdims=True
    )
    return (grad_inputs, gain_grad)


def other_core(values):
    return lax.ppermute(values, "wa", [(0, 1), (1, 0)])


def half_total(partial_value):
    own = partial_value.astype(jnp.bfloat16)
    return own.astype(jnp.float32) + other_core(own).astype(jnp.float32)


def to_parts(values):
    return lax.all_to_all(values, "ctx", 0, 0, tiled=True)


def bucket_hot(rel_local, buckets):
    bucket_count = rel_local.shape[1]
    return (buckets[:, None] == jnp.arange(bucket_count, dtype=jnp.int32)[None, :]).astype(
        jnp.float32
    )


def bias_strips(rel_local, hot, group):
    seq_len = hot.shape[0]
    heads = rel_local.shape[0] // 2
    by_distance = jnp.dot(rel_local, hot.T, precision=HIGHEST)
    by_distance = lax.dynamic_slice_in_dim(by_distance, group * heads, heads, 0)
    ext = jnp.concatenate([jnp.full((heads, TILE), masked_value, jnp.float32), by_distance], 1)
    ext = ext[:, ::-1]
    total = ext.shape[1]
    rows = []
    for diag in range(seq_len // TILE):
        start = total - (diag + 2) * TILE
        strip = ext[:, start : start + 2 * TILE]
        rows.append(jnp.stack([jnp.roll(strip, i, axis=1) for i in range(8)], axis=1))
    return jnp.stack(rows, axis=1)


def bias_grad(skewed, hot, group, head_count):
    heads, diags = skewed.shape[:2]
    seq_len, bucket_count = hot.shape
    sums = sum(jnp.roll(skewed[:, :, i], -i, axis=-1) for i in range(8))
    padded = jnp.concatenate(
        [jnp.zeros((TILE, bucket_count), jnp.float32), hot, jnp.zeros((1, bucket_count), jnp.float32)]
    )[::-1]
    total = padded.shape[0]
    windows = []
    for diag in range(diags):
        low_at = total - 1 - (diag * TILE + TILE)
        high_at = total - 1 - (diag * TILE + 2 * TILE)
        windows.append(padded[low_at : low_at + TILE])
        windows.append(padded[high_at : high_at + TILE])
    spread = jnp.concatenate(windows, axis=0)
    own = jnp.dot(sums.reshape(heads, -1), spread, precision=HIGHEST)
    whole = jnp.zeros((head_count, bucket_count), jnp.float32)
    return lax.dynamic_update_slice_in_dim(whole, own, group * heads, 0)


def fill_bias(strips_ref, bias, head):
    for diag in range(bias.shape[0]):
        strip = strips_ref[head, diag]
        for a in range(TILE // 8):
            shift = (2 * TILE - (TILE - 1 - 8 * a)) % (2 * TILE)
            bias[diag, 8 * a : 8 * a + 8, :] = pltpu.roll(strip, shift, 1)[:, :TILE]


def sort_blocks(where_ref, arrived_ref, held, count):
    parts = held.shape[0]

    @pl.loop(0, count)
    def _(b):
        block = arrived_ref[where_ref[b]]
        for part in range(parts):
            held[part, pl.ds(pl.multiple_of(b * BLK, BLK), BLK), :] = block[
                :, part * HS : (part + 1) * HS
            ]


def rows_of(tile):
    return pl.ds(pl.multiple_of(tile * TILE, TILE), TILE)


def dot_nt(a, b):
    return lax.dot_general(a, b, (((1,), (1,)), ((), ())), preferred_element_type=jnp.float32)


def dot_tn(a, b):
    return lax.dot_general(a, b, (((0,), (0,)), ((), ())), preferred_element_type=jnp.float32)


def forward_kernel(where_ref, arrived_ref, strips_ref, send_ref, mixed_ref, log_ref, held, bias):
    count = arrived_ref.shape[0]
    heads = strips_ref.shape[0]
    tiles = count // PER
    share = where_ref[count]
    sort_blocks(where_ref, arrived_ref, held, count)
    send_ref[...] = jnp.zeros_like(send_ref)

    @pl.loop(0, heads)
    def _(head):
        fill_bias(strips_ref, bias, head)
        for turn in range(2):
            tile = share if turn == 0 else tiles - 1 - share
            query = held[head, rows_of(tile), :]

            def step(j, carry):
                top, total, acc = carry
                key = held[heads + head, rows_of(j), :]
                value = held[2 * heads + head, rows_of(j), :]
                scores = dot_nt(query, key) * 0.125 + bias[tile - j]
                new_top = jnp.maximum(top, jnp.max(scores, axis=1, keepdims=True))
                expo = jnp.exp(scores - new_top)
                keep = jnp.exp(top - new_top)
                total = total * keep + jnp.sum(expo, axis=1, keepdims=True)
                acc = acc * keep + jnp.dot(
                    expo.astype(jnp.bfloat16), value, preferred_element_type=jnp.float32
                )
                return new_top, total, acc

            top, total, acc = lax.fori_loop(
                0,
                tile + 1,
                step,
                (
                    jnp.full((TILE, 1), masked_value, jnp.float32),
                    jnp.zeros((TILE, 1), jnp.float32),
                    jnp.zeros((TILE, HS), jnp.float32),
                ),
            )
            mixed_ref[head, turn * TILE : (turn + 1) * TILE, :] = acc / total
            log_ref[head, turn * TILE : (turn + 1) * TILE, :] = top + jnp.log(total)

    for turn in range(2):
        tile = share if turn == 0 else tiles - 1 - share
        for i in range(PER):
            at = turn * TILE + i * BLK
            block = jnp.concatenate([mixed_ref[h, at : at + BLK, :] for h in range(heads)], axis=1)
            send_ref[where_ref[tile * PER + i]] = block.astype(jnp.bfloat16)


def backward_kernel(
    where_ref,
    arrived_ref,
    strips_ref,
    grad_ref,
    mixed_ref,
    log_ref,
    send_ref,
    skew_ref,
    held,
    grads,
    sums,
    bias,
    score_sum,
):
    count = arrived_ref.shape[0]
    heads = strips_ref.shape[0]
    tiles = count // PER
    share = where_ref[count]
    sort_blocks(where_ref, arrived_ref, held, count)
    sort_blocks(where_ref, grad_ref, grads, count)
    sums[...] = jnp.zeros_like(sums)

    @pl.loop(0, heads)
    def _(head):
        fill_bias(strips_ref, bias, head)
        score_sum[...] = jnp.zeros_like(score_sum)
        for turn in range(2):
            tile = share if turn == 0 else tiles - 1 - share
            query = held[head, rows_of(tile), :]
            grad = grads[head, rows_of(tile), :]
            log_total = log_ref[head, turn * TILE : (turn + 1) * TILE, :]
            mixed = mixed_ref[head, turn * TILE : (turn + 1) * TILE, :]
            delta = jnp.sum(grad.astype(jnp.float32) * mixed, axis=1, keepdims=True)

            @pl.loop(0, tile + 1)
            def _(j):
                key = held[heads + head, rows_of(j), :]
                value = held[2 * heads + head, rows_of(j), :]
                scores = dot_nt(query, key) * 0.125 + bias[tile - j]
                probs = jnp.exp(scores - log_total)
                grad_scores = (probs * (dot_nt(grad, value) - delta)).astype(jnp.bfloat16)
                score_sum[tile - j] += grad_scores.astype(jnp.float32)
                sums[head, rows_of(tile), :] += jnp.dot(
                    grad_scores, key, preferred_element_type=jnp.float32
                )
                sums[heads + head, rows_of(j), :] += dot_tn(grad_scores, query)
                sums[2 * heads + head, rows_of(j), :] += dot_tn(probs.astype(jnp.bfloat16), grad)

        for diag in range(tiles):
            total = jnp.zeros((8, 2 * TILE), jnp.float32)
            for a in range(TILE // 8):
                rows = jnp.concatenate(
                    [score_sum[diag, 8 * a : 8 * a + 8, :], jnp.zeros((8, TILE), jnp.float32)],
                    axis=1,
                )
                total = total + pltpu.roll(rows, (2 * TILE - 8 * a) % (2 * TILE), 1)
            skew_ref[head, diag] = total

    @pl.loop(0, count)
    def _(b):
        at = pl.ds(pl.multiple_of(b * BLK, BLK), BLK)
        parts = [
            sums[part, at, :] * (0.125 if part < 2 * heads else 1.0) for part in range(3 * heads)
        ]
        send_ref[where_ref[b]] = jnp.concatenate(parts, axis=1).astype(jnp.bfloat16)


def kernel_call(body, where, inputs, outs, scratch, cost):
    return pl.pallas_call(
        body,
        in_specs=[pl.BlockSpec(memory_space=pltpu.SMEM)]
        + [pl.BlockSpec(memory_space=pltpu.VMEM)] * len(inputs),
        out_specs=[pl.BlockSpec(memory_space=pltpu.VMEM)] * len(outs),
        out_shape=outs,
        scratch_shapes=scratch,
        compiler_params=pltpu.CompilerParams(vmem_limit_bytes=56 * 1024 * 1024),
        cost_estimate=pl.CostEstimate(flops=cost, bytes_accessed=4000000, transcendentals=1000000),
    )(where, *inputs)


def attention_forward(normed_low, gathered, strips, where):
    width = gathered.shape[1] // 4
    heads = width // HS // 2
    count = lax.axis_size("ctx")
    split = count // SEQS // 2
    cols = heads * HS
    tiles = count // PER
    projected = jnp.dot(
        normed_low, gathered[:, : 3 * width], preferred_element_type=jnp.float32
    ).astype(jnp.bfloat16)
    groups = []
    for g in range(2):
        groups.append(
            jnp.concatenate(
                [
                    projected[:, p * width + g * cols : p * width + (g + 1) * cols]
                    for p in range(3)
                ],
                axis=1,
            ).reshape(SEQS, BLK, 3 * cols)
        )
    outgoing = jnp.broadcast_to(
        jnp.stack(groups, axis=1)[:, :, None], (SEQS, 2, split, BLK, 3 * cols)
    ).reshape(count, BLK, 3 * cols)
    arrived = to_parts(outgoing)
    send, mixed, log_total = kernel_call(
        forward_kernel,
        where,
        (arrived, strips),
        [
            jax.ShapeDtypeStruct((count, BLK, cols), jnp.bfloat16),
            jax.ShapeDtypeStruct((heads, 2 * TILE, HS), jnp.float32),
            jax.ShapeDtypeStruct((heads, 2 * TILE, 1), jnp.float32),
        ],
        [
            pltpu.VMEM((3 * heads, count * BLK, HS), jnp.bfloat16),
            pltpu.VMEM((tiles, TILE, TILE), jnp.float32),
        ],
        heads * (tiles + 1) * TILE * TILE * HS * 4,
    )
    mixed_low = from_parts(send, split).reshape(SEQS, 2, BLK, cols)
    mixed_low = mixed_low.transpose(0, 2, 1, 3).reshape(SEQS * BLK, width)
    branch = half_total(
        lax.dot_general(
            mixed_low,
            gathered[:, 3 * width :],
            (((1,), (1,)), ((), ())),
            preferred_element_type=jnp.float32,
        )
    )
    return (branch, (arrived, mixed, log_total, mixed_low))


def from_parts(send, split):
    parts = to_parts(send)
    count, rows, cols = parts.shape
    parts = parts.reshape(count // split, split, rows, cols)
    return jnp.sum(parts.astype(jnp.float32), axis=1).astype(jnp.bfloat16)


def attention_backward(grad_branch, normed_low, gathered, kept_fwd, strips, where):
    arrived, mixed, log_total, mixed_low = kept_fwd
    width = gathered.shape[1] // 4
    heads = width // HS // 2
    count = lax.axis_size("ctx")
    split = count // SEQS // 2
    cols = heads * HS
    tiles = count // PER
    grad_low = grad_branch.astype(jnp.bfloat16)
    grad_mixed = jnp.dot(
        grad_low, gathered[:, 3 * width :], preferred_element_type=jnp.float32
    ).astype(jnp.bfloat16)
    outgoing = grad_mixed.reshape(SEQS, BLK, 2, cols).transpose(0, 2, 1, 3)
    outgoing = jnp.broadcast_to(
        outgoing[:, :, None], (SEQS, 2, split, BLK, cols)
    ).reshape(count, BLK, cols)
    grad_arrived = to_parts(outgoing)
    output_grad = jnp.einsum("td,te->de", grad_low, mixed_low, preferred_element_type=jnp.float32)
    send, skewed = kernel_call(
        backward_kernel,
        where,
        (arrived, strips, grad_arrived, mixed, log_total),
        [
            jax.ShapeDtypeStruct((count, BLK, 3 * cols), jnp.bfloat16),
            jax.ShapeDtypeStruct((heads, tiles, 8, 2 * TILE), jnp.float32),
        ],
        [
            pltpu.VMEM((3 * heads, count * BLK, HS), jnp.bfloat16),
            pltpu.VMEM((heads, count * BLK, HS), jnp.bfloat16),
            pltpu.VMEM((3 * heads, count * BLK, HS), jnp.float32),
            pltpu.VMEM((tiles, TILE, TILE), jnp.float32),
            pltpu.VMEM((tiles, TILE, TILE), jnp.float32),
        ],
        heads * (tiles + 1) * TILE * TILE * HS * 10,
    )
    back = from_parts(send, split).reshape(SEQS, 2, BLK, 3, cols)
    back = back.transpose(0, 2, 3, 1, 4).reshape(SEQS * BLK, 3 * width)
    grad_partial = lax.dot_general(
        back,
        gathered[:, : 3 * width],
        (((1,), (1,)), ((), ())),
        preferred_element_type=jnp.float32,
    )
    weight_grad = jnp.einsum("td,te->de", normed_low, back, preferred_element_type=jnp.float32)
    weight_grads = jnp.concatenate(
        [weight_grad.astype(jnp.bfloat16), output_grad.astype(jnp.bfloat16)], axis=1
    )
    return (half_total(grad_partial), weight_grads, skewed)


def sum_at_owner(array):
    return lax.psum_scatter(array, "ctx", scatter_dimension=0, tiled=True).astype(jnp.float32)


def dot_back(a, b):
    return lax.dot_general(a, b, (((1,), (1,)), ((), ())), preferred_element_type=jnp.float32)


def gelu_back(pre_act, grad_hidden):
    _, gelu_pull = jax.vjp(gelu_fn, pre_act)
    return gelu_pull(grad_hidden)[0].astype(jnp.bfloat16)


def expert_block(normed, routes, router, expert_up, expert_down, grad_out):
    normed_low = normed.astype(jnp.bfloat16)
    tok_rows, top_count = routes.shape
    num_experts = router.shape[1]
    width = normed.shape[1]
    capacity = 2 * tok_rows * top_count // num_experts
    half = capacity // 2
    expert_up = expert_up[0]
    expert_down = expert_down[0]
    expert_ids = jnp.arange(num_experts, dtype=jnp.int32)
    flat_routes = routes.reshape(-1)
    items = flat_routes.shape[0]
    one_hot = flat_routes[:, None] == expert_ids[None, :]
    order = jnp.arange(items, dtype=jnp.int32)
    earlier = (order[:, None] > order[None, :]).astype(jnp.bfloat16)
    ranks = jnp.dot(earlier, one_hot.astype(jnp.bfloat16), preferred_element_type=jnp.float32)
    slot_rank = jnp.sum(jnp.where(one_hot, ranks, 0.0), axis=1).astype(jnp.int32)
    rank_here = slot_rank - half * lax.axis_index("wa")
    inside = (rank_here >= 0) & (rank_here < half)
    place = jnp.where(inside, flat_routes * half + rank_here, -1)
    slots = num_experts * half
    pick = (place[:, None] == jnp.arange(slots, dtype=jnp.int32)[None, :]).astype(jnp.bfloat16)
    logits = jnp.dot(normed, router, precision=HIGHEST)
    route_hot = (routes[..., None] == expert_ids[None, None, :]).astype(jnp.float32)
    chosen_logits = jnp.sum(logits[:, None, :] * route_hot, axis=-1)
    gate_probs = jax.nn.softmax(chosen_logits, axis=-1)
    grad_choice = (gate_probs[..., None] * grad_out[:, None, :]).astype(jnp.bfloat16)
    both = jnp.concatenate(
        [jnp.repeat(normed_low, top_count, axis=0), grad_choice.reshape(items, width)], axis=1
    )
    outgoing = lax.dot_general(
        pick, both, (((0,), (0,)), ((), ())), preferred_element_type=jnp.float32
    ).astype(jnp.bfloat16)
    here = to_parts(outgoing.reshape(num_experts, half, 2 * width)).reshape(slots, 2 * width)
    rows = jnp.concatenate([here, other_core(here)], axis=0)
    inputs = rows[:, :width]
    grad_rows = rows[:, width:]
    pre_act = jnp.dot(inputs, expert_up, preferred_element_type=jnp.float32)
    hidden = gelu_fn(pre_act).astype(jnp.bfloat16)
    part = jnp.dot(hidden, expert_down, preferred_element_type=jnp.float32).astype(jnp.bfloat16)
    grad_pre = gelu_back(pre_act, dot_back(grad_rows, expert_down))
    grad_part = dot_back(grad_pre, expert_up).astype(jnp.bfloat16)
    parts = jnp.concatenate([part, grad_part], axis=1)
    totals = (
        parts[:slots].astype(jnp.float32) + other_core(parts[slots:]).astype(jnp.float32)
    ).astype(jnp.bfloat16)
    back = to_parts(totals.reshape(num_experts, half, 2 * width)).reshape(slots, 2 * width)
    down_grad = jnp.einsum("cf,cd->fd", hidden, grad_rows, preferred_element_type=jnp.float32)
    up_grad = jnp.einsum("cd,cf->df", inputs, grad_pre, preferred_element_type=jnp.float32)
    chosen = jnp.dot(pick, back[:, :width], preferred_element_type=jnp.float32)
    pick_token = jnp.sum(
        pick.astype(jnp.float32).reshape(tok_rows, top_count, slots), axis=1
    ).astype(jnp.bfloat16)
    grad_token = jnp.dot(pick_token, back[:, width:], preferred_element_type=jnp.float32)
    joined = half_total(jnp.concatenate([chosen, grad_token], axis=0))
    per_choice = joined[:items].reshape(tok_rows, top_count, width)
    mixture = jnp.sum(gate_probs[..., None] * per_choice, axis=1)
    grad_gate = jnp.sum(grad_out[:, None, :] * per_choice, axis=-1)
    grad_chosen = gate_probs * (grad_gate - jnp.sum(gate_probs * grad_gate, axis=-1, keepdims=True))
    grad_logits = jnp.sum(grad_chosen[..., None] * route_hot, axis=1)
    router_grad = jnp.dot(normed.T, grad_logits, precision=HIGHEST)
    grad_from_router = jnp.dot(grad_logits, router.T, precision=HIGHEST)
    grad_normed = joined[items:] + grad_from_router
    return (mixture, grad_normed, router_grad, up_grad[None], down_grad[None])


def sum_everywhere(arrays):
    flat = jnp.concatenate([a.reshape(-1) for a in arrays])
    flat = lax.psum(flat, "ctx")
    out, at = ([], 0)
    for a in arrays:
        out.append(flat[at : at + a.size].reshape(a.shape))
        at += a.size
    return out


def local(
    tokens,
    cotangent,
    routes,
    buckets,
    block_order,
    attend_gain1,
    rel_bias1,
    query_proj1,
    key_proj1,
    value_proj1,
    output_proj1,
    dense_gain1,
    dense_up1,
    dense_down1,
    attend_gain2,
    rel_bias2,
    query_proj2,
    key_proj2,
    value_proj2,
    output_proj2,
    expert_gain2,
    router,
    expert_up,
    expert_down,
):
    count = lax.axis_size("ctx")
    split = count // SEQS // 2
    here = lax.axis_index("ctx")
    group = (here // split) % 2
    ids = jnp.arange(count, dtype=jnp.int32)
    place_of = jnp.sum(jnp.where(block_order[:, None] == ids[None, :], ids[:, None], 0), axis=0)
    where = jnp.concatenate([place_of, (here % split)[None].astype(jnp.int32)])
    head_count = rel_bias1.shape[0]
    width = query_proj1.shape[1]
    gathered_one = lax.all_gather(
        jnp.concatenate([query_proj1, key_proj1, value_proj1, output_proj1], axis=1),
        "ctx",
        axis=0,
        tiled=True,
    )
    dense_full = lax.all_gather(
        jnp.concatenate([dense_up1, dense_down1], axis=1), "ctx", axis=0, tiled=True
    )
    gathered_two = lax.all_gather(
        jnp.concatenate([query_proj2, key_proj2, value_proj2, output_proj2], axis=1),
        "ctx",
        axis=0,
        tiled=True,
    )
    hidden_width = dense_up1.shape[1]
    up_full = dense_full[:, :hidden_width]
    down_full = dense_full[:, hidden_width:]
    hot = bucket_hot(rel_bias1, buckets)
    strips_one = bias_strips(rel_bias1, hot, group)
    strips_two = bias_strips(rel_bias2, hot, group)
    residual = tokens.astype(jnp.float32)
    normed_a1, inv_a1 = rms_norm(residual, attend_gain1)
    low_a1 = normed_a1.astype(jnp.bfloat16)
    branch_a1, kept_a1 = attention_forward(low_a1, gathered_one, strips_one, where)
    after_attn1 = residual + branch_a1
    normed_d1, inv_d1 = rms_norm(after_attn1, dense_gain1)
    low_d1 = normed_d1.astype(jnp.bfloat16)
    pre_d1 = jnp.dot(low_d1, up_full, preferred_element_type=jnp.float32)
    hidden_d1 = gelu_fn(pre_d1).astype(jnp.bfloat16)
    after_dense1 = after_attn1 + half_total(dot_back(hidden_d1, down_full))
    normed_a2, inv_a2 = rms_norm(after_dense1, attend_gain2)
    low_a2 = normed_a2.astype(jnp.bfloat16)
    branch_a2, kept_a2 = attention_forward(low_a2, gathered_two, strips_two, where)
    after_attn2 = after_dense1 + branch_a2
    normed_e2, inv_e2 = rms_norm(after_attn2, expert_gain2)
    grad_out = cotangent.astype(jnp.float32)
    mixture, grad_normed_e2, router_grad, up_grad, down_grad = expert_block(
        normed_e2, routes, router, expert_up, expert_down, grad_out
    )
    result = (after_attn2 + mixture).astype(jnp.bfloat16)
    grad_part, gain_e2 = norm_back(after_attn2, inv_e2, expert_gain2, grad_normed_e2)
    grad_residual = grad_out + grad_part
    grad_normed_a2, grads_two, skewed_two = attention_backward(
        grad_residual, low_a2, gathered_two, kept_a2, strips_two, where
    )
    own_two = sum_at_owner(grads_two)
    grad_part, gain_a2 = norm_back(after_dense1, inv_a2, attend_gain2, grad_normed_a2)
    grad_residual = grad_residual + grad_part
    grad_low = grad_residual.astype(jnp.bfloat16)
    down_part = jnp.einsum("td,tf->df", grad_low, hidden_d1, preferred_element_type=jnp.float32)
    grad_hidden = jnp.dot(grad_low, down_full, preferred_element_type=jnp.float32)
    grad_pre = gelu_back(pre_d1, grad_hidden)
    up_part = jnp.einsum("td,tf->df", low_d1, grad_pre, preferred_element_type=jnp.float32)
    grad_normed_d1 = half_total(dot_back(grad_pre, up_full))
    own_dense = sum_at_owner(
        jnp.concatenate([up_part.astype(jnp.bfloat16), down_part.astype(jnp.bfloat16)], axis=1)
    )
    grad_part, gain_d1 = norm_back(after_attn1, inv_d1, dense_gain1, grad_normed_d1)
    grad_residual = grad_residual + grad_part
    rel_two = bias_grad(skewed_two, hot, group, head_count)
    gain_d1, gain_a2, gain_e2, rel_two, router_grad = sum_everywhere(
        [gain_d1, gain_a2, gain_e2, rel_two, router_grad]
    )
    grad_normed_a1, grads_one, skewed_one = attention_backward(
        grad_residual, low_a1, gathered_one, kept_a1, strips_one, where
    )
    own_one = sum_at_owner(grads_one)
    grad_part, gain_a1 = norm_back(residual, inv_a1, attend_gain1, grad_normed_a1)
    grad_tokens = grad_residual + grad_part
    rel_one = bias_grad(skewed_one, hot, group, head_count)
    gain_a1, rel_one = sum_everywhere([gain_a1, rel_one])
    query_one, key_one, value_one, output_one = jnp.split(own_one, 4, axis=1)
    query_two, key_two, value_two, output_two = jnp.split(own_two, 4, axis=1)
    return (
        result,
        grad_tokens,
        gain_a1,
        rel_one,
        query_one,
        key_one,
        value_one,
        output_one,
        gain_d1,
        own_dense[:, :hidden_width],
        own_dense[:, hidden_width:],
        gain_a2,
        rel_two,
        query_two,
        key_two,
        value_two,
        output_two,
        gain_e2,
        router_grad,
        up_grad,
        down_grad,
    )


def solution(mesh):
    placed = (
        P("ctx", None),
        P("ctx", None),
        P("ctx", None),
        P(),
        P(),
        P(),
        P("wa", None),
        P("ctx", "wa"),
        P("ctx", "wa"),
        P("ctx", "wa"),
        P("ctx", "wa"),
        P(),
        P("ctx", "wa"),
        P("ctx", "wa"),
        P(),
        P("wa", None),
        P("ctx", "wa"),
        P("ctx", "wa"),
        P("ctx", "wa"),
        P("ctx", "wa"),
        P(),
        P(),
        P("ctx", None, "wa"),
        P("ctx", "wa", None),
    )
    return jax.shard_map(
        local,
        mesh=mesh,
        in_specs=placed,
        out_specs=(
            P("ctx", None),
            P("ctx", None),
            P(),
            P("wa", None),
            P("ctx", "wa"),
            P("ctx", "wa"),
            P("ctx", "wa"),
            P("ctx", "wa"),
            P(),
            P("ctx", "wa"),
            P("ctx", "wa"),
            P(),
            P("wa", None),
            P("ctx", "wa"),
            P("ctx", "wa"),
            P("ctx", "wa"),
            P("ctx", "wa"),
            P(),
            P(),
            P("ctx", None, "wa"),
            P("ctx", "wa", None),
        ),
        check_vma=False,
    )
```

time: 2260 us -> 1050 us (0.46)
  waiting for transfers between devices: 947 us -> 406 us
  local copies, waits for them, and re-layouts: 477 us -> 173 us
  blocking collectives: 426 us -> 222 us
  matrix products: 223 us -> 75.1 us
  Pallas kernels: 0 us -> 59.8 us
  loops' own time: 32.4 us -> 0 us
  starting transfers between devices: 58.6 us -> 33.3 us
    reduce_scatter x4 -> x3, waiting for transfers between devices: 559 us -> 196 us  [sum_at_owner(): lax.psum_scatter(array, 'ctx', scatter_dimension=0, tiled=True)]
    all_gather x8 -> x0, blocking collectives: 348 us -> none  [the longest x2 90.5 us: gather_attention(): lax.all_gather(weights[2], 'ctx', axis=0, tiled=True)]
    dot_general x99 -> x27, matrix products: 210 us -> 62.3 us  [the longest x4 11.9 us: dot_back(): lax.dot_general(a, b, (((1,), (1,)), ((), ())), preferred_element_type=jn...]
    all_to_all x0 -> x5, blocking collectives: none -> 145 us  [to_parts(): return lax.all_to_all(values, 'ctx', 0, 0, tiled=True)]
    reshape x53 -> x16, local copies, waits for them, and re-layouts: 127 us -> 17 us  [the longest x2 3.84 us: attention_backward(): back = from_parts(send, split).reshape(SEQS, 2, BLK, 3, cols)]
    psum x7 -> x0, waiting for transfers between devices: 107 us -> none  [half_total(): lax.psum(partial_value.astype(jnp.bfloat16), 'wa').astype(jnp.float32)]
    dynamic_slice x41 -> x1, local copies, waits for them, and re-layouts: 73.9 us -> 0.01 us  [bias_strips(): by_distance = lax.dynamic_slice_in_dim(by_distance, group * heads, heads, 0)]
    dynamic_update_slice x40 -> x2, local copies, waits for them, and re-layouts: 69.8 us -> 0.23 us  [bias_grad(): return lax.dynamic_update_slice_in_dim(whole, own, group * heads, 0)]
  transfers between devices with their start and end apart: 24 -> 20, of which waited for: 17 -> 15; matrix products, arithmetic and copies ran while one was open for 11% -> 21% of each run, Pallas kernels for 0% -> 3%
where the time goes in v1:
time: 1050 us; the launch traced here: 1040 us
  waiting for transfers between devices  406 us (39%)
  blocking collectives  222 us (21%)
  local copies, waits for them, and re-layouts  173 us (16%)
  matrix products  75.1 us (7%)
  Pallas kernels  59.8 us (6%)
  other arithmetic  54.8 us (5%)
  starting transfers between devices  33.3 us (3%)
  between operations  16.4 us (2%)
    reduce_scatter x3, waiting for transfers between devices, sum_at_owner(): lax.psum_scatter(array, 'ctx', scatter_dimension=0, tiled=True)  196 us
    all_to_all x5, blocking collectives, to_parts(): return lax.all_to_all(values, 'ctx', 0, 0, tiled=True)  145 us
    all_to_all x5, waiting for transfers between devices, to_parts(): return lax.all_to_all(values, 'ctx', 0, 0, tiled=True)  101 us
    unnamed x341, local copies, waits for them, and re-layouts  84.5 us
    psum x1, blocking collectives, sum_everywhere(): flat = lax.psum(flat, 'ctx')  77.4 us
    pallas_call x4, Pallas kernels, kernel_call(): pl.pallas_call(body, in_specs=[pl.BlockSpec(memory_space=pltpu.SMEM)] + [...  59.8 us
    all_gather x1, waiting for transfers between devices, local(): lax.all_gather(jnp.concatenate([query_proj2, key_proj2, value_proj2, outp...  56.6 us
    all_gather x1, waiting for transfers between devices, local(): lax.all_gather(jnp.concatenate([query_proj1, key_proj1, value_proj1, outp...  37.5 us
  transfers between devices with their start and end apart: 20, of which 15 were waited for; matrix products, arithmetic and copies ran while one was open for 21% of the time, Pallas kernels for 3%

profile of v1, /device:TPU:0, one launch (start us, length us, event | category | flops | bytes accessed | tf_op | source)
XLA Modules:
  0.0 1040.8 jit_solution(7448224347098882089)
XLA Ops:
  39.2 37.5 %all-gather.4.cloned.1.call-done = bf16[768,1536]{1,0:T(8,128)(2,1)} async-done(((bf16[48,1536]{1,0:T(8,128)(2,1)}), bf16[768,1536]{1,0:T(8,128)(2,1)}) %all-gather.4.cloned.1.call-update) | async-done | bytes 2359312 | tf_op jit(solution)/shard_map/all_gather | solution.py:491
  80.8 4.5 all-to-all-start
  94.7 32.9 %all-to-all-done.arrived_ref = bf16[16,64,576]{2,1,0:T(8,128)(2,1)} async-done(((bf16[16,64,576]{2,1,0:T(8,128)(2,1)}), bf16[16,64,576]{2,1,0:T(8,128)(2,1)}, u32[]{:S(2)}, u32[]{:S(2)}) %all-to-all-start) | async-done | bytes 1179680 | tf_op jit(solution)/shard_map/all_to_all | solution.py:48
  127.6 12.2 %shard_map.391 = (bf16[16,64,192]{2,1,0:T(8,128)(2,1)}, f32[3,512,64]{2,1,0:T(8,128)}, f32[3,512,1]{2,1,0:T(8,128)}) custom-call(s32[17]{0:T(128)} %pad_add_fusion.where_ref, bf16[16,64,576]{2,1,0:T(8,128)(2,1)} %all-to-all-done.arrived_ref, f32[3,4,8,512]{3,2,1,0:T(8,128)} %pad_maximum_fusion.15.strips_ref), custom_call_target="tpu_custom_call" | custom-call | flops 251658240 | bytes 4000000 | tf_op jit(solution)/shard_map/pallas_call | solution.py:245
  139.8 13.0 %all-to-all-start.1 = ((bf16[16,64,192]{2,1,0:T(8,128)(2,1)}), bf16[16,64,192]{2,1,0:T(8,128)(2,1)S(1)}, u32[]{:S(2)}, u32[]{:S(2)}) async-start(bf16[16,64,192]{2,1,0:T(8,128)(2,1)} %get-tuple-element.31), calls=%async_computation.1 | async-start | bytes 1048576 | tf_op jit(solution)/shard_map/all_to_all | solution.py:48
  166.8 8.0 all-to-all-done.1
  188.5 56.6 %all-gather.8.cloned.1.call-done = bf16[768,1536]{1,0:T(8,128)(2,1)} async-done(((bf16[48,1536]{1,0:T(8,128)(2,1)}), bf16[768,1536]{1,0:T(8,128)(2,1)}) %all-gather.8.cloned.1.call-update) | async-done | bytes 2359312 | tf_op jit(solution)/shard_map/all_gather | solution.py:500
  249.4 4.5 all-to-all-start.2
  256.7 2.7 slice.1246
  259.4 2.7 reverse.167
  263.4 2.7 reverse.168
  268.8 2.7 reverse.169
  274.2 2.7 reverse.170
  284.9 2.7 reverse.172
  290.2 2.7 reverse.173
  304.2 2.7 reverse.175
  307.7 2.7 reverse.176
  311.7 2.7 reverse.177
  315.8 2.7 reverse.178
  323.8 2.7 reverse.180
  335.0 12.2 %shard_map.392 = (bf16[16,64,192]{2,1,0:T(8,128)(2,1)}, f32[3,512,64]{2,1,0:T(8,128)}, f32[3,512,1]{2,1,0:T(8,128)}) custom-call(s32[17]{0:T(128)} %pad_add_fusion.where_ref, bf16[16,64,576]{2,1,0:T(8,128)(2,1)} %all-to-all-done.2.arrived_ref, f32[3,4,8,512]{3,2,1,0:T(8,128)} %pad_maximum_fusion.16.strips_ref), custom_call_target="tpu_custom_call" | custom-call | flops 251658240 | bytes 4000000 | tf_op jit(solution)/shard_map/pallas_call | solution.py:245
  347.2 22.1 %all_to_all.50 = bf16[16,64,192]{2,1,0:T(8,128)(2,1)S(1)} all-to-all(bf16[16,64,192]{2,1,0:T(8,128)(2,1)} %get-tuple-element.32), channel_id=1, replica_groups=mesh['ctx'=16,'wa'=2] {'ctx'}, dimensions={0} | all-to-all | bytes 786432 | tf_op jit(solution)/shard_map/all_to_all | solution.py:48
  378.9 3.1 mul.470
  392.4 3.0 reshape.369
  398.8 41.9 %all_to_all.51 = bf16[16,32,1536]{2,1,0:T(8,128)(2,1)S(1)} all-to-all(bf16[16,32,1536]{2,1,0:T(8,128)(2,1)S(1)} %bitcast.420), channel_id=1, replica_groups=mesh['ctx'=16,'wa'=2] {'ctx'}, dimensions={0} | all-to-all | bytes 3145728 | tf_op jit(solution)/shard_map/all_to_all | solution.py:48
  440.7 3.4 collective-permute-done.3
  446.8 3.4 fusion.28
  450.2 6.6 fusion.6
  459.8 3.3 collective-permute-done.4
  465.4 4.4 all-to-all-start.5
  471.3 32.7 %all-to-all-done.5 = bf16[16,32,1536]{2,1,0:T(8,128)(2,1)S(1)} async-done(((bf16[16,32,1536]{2,1,0:T(8,128)(2,1)}), bf16[16,32,1536]{2,1,0:T(8,128)(2,1)S(1)}, u32[]{:S(2)}, u32[]{:S(2)}) %all-to-all-start.5) | async-done | bytes 1572896 | tf_op jit(solution)/shard_map/all_to_all | solution.py:48
  506.9 2.8 collective-permute-done.5
  512.9 3.6 multiply_reduce_fusion.2
  519.4 2.9 multiply_reduce_fusion.1
  526.3 23.3 %all_to_all.52.grad_ref = bf16[16,64,192]{2,1,0:T(8,128)(2,1)} all-to-all(bf16[16,64,192]{2,1,0:T(8,128)(2,1)S(1)} %bitcast.416), channel_id=1, replica_groups=mesh['ctx'=16,'wa'=2] {'ctx'}, dimensions={0} | all-to-all | bytes 786432 | tf_op jit(solution)/shard_map/all_to_all | solution.py:48
  549.6 17.7 %shard_map.393 = (bf16[16,64,576]{2,1,0:T(8,128)(2,1)}, f32[3,4,8,512]{3,2,1,0:T(8,128)}) custom-call(s32[17]{0:T(128)} %pad_add_fusion.where_ref, bf16[16,64,576]{2,1,0:T(8,128)(2,1)} %all-to-all-done.2.arrived_ref, f32[3,4,8,512]{3,2,1,0:T(8,128)} %pad_maximum_fusion.16.strips_ref, bf16[16,64,192]{2,1,0:T(8,128)(2,1)} %all_to_all.52.grad_ref, ...), custom_call_target="tpu_custom_call" | custom-call | flops 629145600 | bytes 4000000 | tf_op jit(solution)/shard_map/pallas_call | solution.py:245
  567.3 36.0 %all_to_all.53 = bf16[16,64,576]{2,1,0:T(8,128)(2,1)S(1)} all-to-all(bf16[16,64,576]{2,1,0:T(8,128)(2,1)} %get-tuple-element.35), channel_id=1, replica_groups=mesh['ctx'=16,'wa'=2] {'ctx'}, dimensions={0} | all-to-all | bytes 2359296 | tf_op jit(solution)/shard_map/all_to_all | solution.py:48
  614.2 3.5 fusion.37
  628.0 21.7 %all_to_all.54.grad_ref = bf16[16,64,192]{2,1,0:T(8,128)(2,1)} all-to-all(bf16[16,64,192]{2,1,0:T(8,128)(2,1)S(1)} %bitcast.417), channel_id=1, replica_groups=mesh['ctx'=16,'wa'=2] {'ctx'}, dimensions={0} | all-to-all | bytes 786432 | tf_op jit(solution)/shard_map/all_to_all | solution.py:48
  649.7 17.7 %shard_map.394 = (bf16[16,64,576]{2,1,0:T(8,128)(2,1)}, f32[3,4,8,512]{3,2,1,0:T(8,128)}) custom-call(s32[17]{0:T(128)} %pad_add_fusion.where_ref, bf16[16,64,576]{2,1,0:T(8,128)(2,1)} %all-to-all-done.arrived_ref, f32[3,4,8,512]{3,2,1,0:T(8,128)} %pad_maximum_fusion.15.strips_ref, bf16[16,64,192]{2,1,0:T(8,128)(2,1)} %all_to_all.54.grad_ref, ...), custom_call_target="tpu_custom_call" | custom-call | flops 629145600 | bytes 4000000 | tf_op jit(solution)/shard_map/pallas_call | solution.py:245
  667.4 5.4 all-to-all-start.9
  674.6 27.6 %all-to-all-done.9 = bf16[16,64,576]{2,1,0:T(8,128)(2,1)} async-done(((bf16[16,64,576]{2,1,0:T(8,128)(2,1)}), bf16[16,64,576]{2,1,0:T(8,128)(2,1)}, u32[]{:S(2)}, u32[]{:S(2)}) %all-to-all-start.9) | async-done | bytes 1179680 | tf_op jit(solution)/shard_map/all_to_all | solution.py:48
  718.2 2.7 pad_maximum_fusion
  722.8 7.3 convolution_bitcast_fusion.1
  730.1 8.7 convolution_bitcast_fusion
  748.8 77.4 %all-reduce.18 = (f32[960]{0:T(1024)S(1)}, f32[14784]{0:T(1024)S(1)}) all-reduce(f32[960]{0:T(1024)S(1)} %pad_maximum_fusion.21, f32[14784]{0:T(1024)S(1)} %concatenate.425), channel_id=1, replica_groups=mesh['ctx'=16,'wa'=2] {'ctx'}, use_global_device_ids=true, to_apply=%region_23.24 | all-reduce | flops 15744 | bytes 125952 | tf_op jit(solution)/shard_map/psum | solution.py:448
  833.9 55.8 %reduce-scatter.4.cloned.1.call-done = bf16[48,1536]{1,0:T(8,128)(2,1)} async-done(((bf16[768,1536]{1,0:T(8,128)(2,1)}), bf16[48,1536]{1,0:T(8,128)(2,1)}) %reduce-scatter.4.cloned.1.call-update) | async-done | bytes 147472 | tf_op jit(solution)/shard_map/reduce_scatter | solution.py:368
  891.2 140.7 %reduce-scatter.6.cloned.1.call-done = bf16[48,3072]{1,0:T(8,128)(2,1)} async-done(((bf16[768,3072]{1,0:T(8,128)(2,1)}), bf16[48,3072]{1,0:T(8,128)(2,1)}) %reduce-scatter.6.cloned.1.call-update) | async-done | bytes 294928 | tf_op jit(solution)/shard_map/reduce_scatter | solution.py:368
  (692 shorter events, 232.3 us)
Async XLA Ops:
  7.2 439.5 %copy-start = (bf16[1,1536,768]{2,1,0:T(8,128)(2,1)S(1)}, bf16[1,1536,768]{2,1,0:T(8,128)(2,1)}, u32[]{:S(2)}) copy-start(bf16[1,1536,768]{2,1,0:T(8,128)(2,1)} %param.47) | copy-start | bytes 7077892
  7.2 11.4 %copy-start.9 = (bf16[256,768]{1,0:T(8,128)(2,1)S(1)}, bf16[256,768]{1,0:T(8,128)(2,1)}, u32[]{:S(2)}) copy-start(bf16[256,768]{1,0:T(8,128)(2,1)} %param.24) | copy-start | bytes 1179652
  7.2 69.5 %all-gather.4.cloned.1.call-start = ((), (), s32[]{:S(2)}) async-start(), calls=%async_computation.13 | async-start | bytes 2506752 | tf_op jit(solution)/shard_map/all_gather | solution.py:491
  9.0 171.4 %all-gather.6.cloned.1.call-start = ((), (), s32[]{:S(2)}) async-start(), calls=%async_computation.14 | async-start | bytes 5013504 | tf_op jit(solution)/shard_map/all_gather | solution.py:497
  10.7 66.0 %copy-start.52 = (f32[768]{0:T(1024)S(1)}, f32[768]{0:T(1024)}, u32[]{:S(2)}) copy-start(f32[768]{0:T(1024)} %param.29) | copy-start | bytes 9220
  10.8 234.3 %all-gather.8.cloned.1.call-start = ((), (), s32[]{:S(2)}) async-start(), calls=%async_computation.15 | async-start | bytes 2506752 | tf_op jit(solution)/shard_map/all_gather | solution.py:500
  18.7 60.2 %copy-start.65 = (f32[256]{0:T(256)}, f32[256]{0:T(256)S(1)}, u32[]{:S(2)}) copy-start(f32[256]{0:T(256)S(1)} %add_rsqrt_fusion.3) | copy-start | bytes 3076
  79.6 12.5 %copy-start.82 = (s32[16]{0:T(128)S(1)}, s32[16]{0:T(128)}, u32[]{:S(2)}) copy-start(s32[16]{0:T(128)} %param.28) | copy-start | bytes 196
  80.8 46.8 %all-to-all-start = ((bf16[16,64,576]{2,1,0:T(8,128)(2,1)}), bf16[16,64,576]{2,1,0:T(8,128)(2,1)}, u32[]{:S(2)}, u32[]{:S(2)}) async-start(bf16[16,64,576]{2,1,0:T(8,128)(2,1)} %bitcast.413), calls=%async_computation | async-start | bytes 2621440 | tf_op jit(solution)/shard_map/all_to_all | solution.py:48
  85.3 73.0 %copy-start.78 = (f32[3,2]{1,0:T(4,128)S(1)}, f32[3,2]{1,0:T(4,128)}, u32[]{:S(2)}) copy-start(f32[3,2]{1,0:T(4,128)} %get-tuple-element.242) | copy-start | bytes 76
  139.8 35.0 %all-to-all-start.1 = ((bf16[16,64,192]{2,1,0:T(8,128)(2,1)}), bf16[16,64,192]{2,1,0:T(8,128)(2,1)S(1)}, u32[]{:S(2)}, u32[]{:S(2)}) async-start(bf16[16,64,192]{2,1,0:T(8,128)(2,1)} %get-tuple-element.31), calls=%async_computation.1 | async-start | bytes 1048576 | tf_op jit(solution)/shard_map/all_to_all | solution.py:48
  166.8 13.5 %copy-start.41 = (f32[768]{0:T(1024)S(1)}, f32[768]{0:T(1024)}, u32[]{:S(2)}) copy-start(f32[768]{0:T(1024)} %param.35) | copy-start | bytes 9220
  176.9 1.8 collective-permute-start
  184.6 60.5 %copy-start.50 = (f32[768]{0:T(1024)S(1)}, f32[768]{0:T(1024)}, u32[]{:S(2)}) copy-start(f32[768]{0:T(1024)} %param.38) | copy-start | bytes 9220
  184.6 2.8 collective-permute-start.1
  188.5 59.2 %copy-start.68 = (f32[256]{0:T(256)}, f32[256]{0:T(256)S(1)}, u32[]{:S(2)}) copy-start(f32[256]{0:T(256)S(1)} %add_rsqrt_fusion.1) | copy-start | bytes 3076
  248.2 55.7 %copy-start.60 = (f32[3,511]{1,0:T(4,128)S(1)}, f32[3,511]{1,0:T(4,128)}, u32[]{:S(2)}) copy-start(f32[3,511]{1,0:T(4,128)} %get-tuple-element.217) | copy-start | bytes 18400
  249.4 85.6 %all-to-all-start.2 = ((bf16[16,64,576]{2,1,0:T(8,128)(2,1)}), bf16[16,64,576]{2,1,0:T(8,128)(2,1)}, u32[]{:S(2)}, u32[]{:S(2)}) async-start(bf16[16,64,576]{2,1,0:T(8,128)(2,1)} %bitcast.412), calls=%async_computation.2 | async-start | bytes 2621440 | tf_op jit(solution)/shard_map/all_to_all | solution.py:48
  347.2 27.3 %copy-start.59 = (s32[256,2]{0,1:T(2,128)S(1)}, s32[256,2]{0,1:T(2,128)}, u32[]{:S(2)}) copy-start(s32[256,2]{0,1:T(2,128)} %param.26) | copy-start | bytes 6148
  374.5 8.4 collective-permute-start.2
  378.9 5.6 copy-start.43
  398.8 45.3 %copy-start.81 = (bf16[1,768,1536]{2,1,0:T(8,128)(2,1)S(1)}, bf16[1,768,1536]{2,1,0:T(8,128)(2,1)}, u32[]{:S(2)}) copy-start(bf16[1,768,1536]{2,1,0:T(8,128)(2,1)} %param.46) | copy-start | bytes 7077892
  440.7 9.5 copy-start.10
  440.7 3.4 collective-permute-start.3
  444.1 6.0 copy-start.30
  459.7 3.5 collective-permute-start.4
  465.4 4.8 copy-start.73
  465.4 38.6 %all-to-all-start.5 = ((bf16[16,32,1536]{2,1,0:T(8,128)(2,1)}), bf16[16,32,1536]{2,1,0:T(8,128)(2,1)S(1)}, u32[]{:S(2)}, u32[]{:S(2)}) async-start(bf16[16,32,1536]{2,1,0:T(8,128)(2,1)} %bitcast.89), calls=%async_computation.5 | async-start | bytes 3145728 | tf_op jit(solution)/shard_map/all_to_all | solution.py:48
  469.8 362.6 %reduce-scatter.8.cloned.1.call-start = ((), (), s32[]{:S(2)}) async-start(), calls=%async_computation.18 | async-start | bytes 2506752 | tf_op jit(solution)/shard_map/reduce_scatter | solution.py:368
  506.8 2.9 collective-permute-start.5
  611.1 1.8 collective-permute-start.6
  619.4 2.6 collective-permute-start.7
  626.0 47.3 %copy-start.7 = (f32[256,768]{1,0:T(8,128)}, f32[256,768]{1,0:T(8,128)S(1)}, u32[]{:S(2)}) copy-start(f32[256,768]{1,0:T(8,128)S(1)} %subtract_add_fusion) | copy-start | bytes 2359300
  649.7 23.7 %copy-start.22 = (bf16[256,384]{1,0:T(8,128)(2,1)S(1)}, bf16[256,384]{1,0:T(8,128)(2,1)}, u32[]{:S(2)}) copy-start(bf16[256,384]{1,0:T(8,128)(2,1)} %copy-done.21) | copy-start | bytes 589828
  667.4 34.8 %all-to-all-start.9 = ((bf16[16,64,576]{2,1,0:T(8,128)(2,1)}), bf16[16,64,576]{2,1,0:T(8,128)(2,1)}, u32[]{:S(2)}, u32[]{:S(2)}) async-start(bf16[16,64,576]{2,1,0:T(8,128)(2,1)} %get-tuple-element.38), calls=%async_computation.9 | async-start | bytes 2621440 | tf_op jit(solution)/shard_map/all_to_all | solution.py:48
  672.8 216.9 %reduce-scatter.4.cloned.1.call-start = ((), (), s32[]{:S(2)}) async-start(), calls=%async_computation.16 | async-start | bytes 2506752 | tf_op jit(solution)/shard_map/reduce_scatter | solution.py:368
  704.8 7.2 copy-start.53
  704.8 7.2 copy-start.66
  714.4 317.4 %reduce-scatter.6.cloned.1.call-start = ((), (), s32[]{:S(2)}) async-start(), calls=%async_computation.17 | async-start | bytes 5013504 | tf_op jit(solution)/shard_map/reduce_scatter | solution.py:368
  722.8 19.3 %copy-start.32 = (f32[2048,32]{0,1:T(8,128)}, f32[2048,32]{0,1:T(8,128)S(1)}, u32[]{:S(2)}) copy-start(f32[2048,32]{0,1:T(8,128)S(1)} %constant_dynamic-update-slice_fusion.48) | copy-start | bytes 786436
  722.8 7.3 copy-start.31
  730.1 8.7 copy-start.45
  730.1 8.7 copy-start.58
  730.1 10.4 %copy-start.39 = (f32[3,4,8,512]{3,2,1,0:T(8,128)S(1)}, f32[3,4,8,512]{3,2,1,0:T(8,128)}, u32[]{:S(2)}) copy-start(f32[3,4,8,512]{3,2,1,0:T(8,128)} %get-tuple-element.40) | copy-start | bytes 589828
  746.2 83.9 %copy-start.8 = (f32[256,768]{1,0:T(8,128)S(1)}, f32[256,768]{1,0:T(8,128)}, u32[]{:S(2)}) copy-start(f32[256,768]{1,0:T(8,128)} %copy-done.7) | copy-start | bytes 2359300
  746.2 1.8 collective-permute-start.8
  826.2 65.0 %copy-start.80 = (f32[960]{0:T(1024)}, f32[960]{0:T(1024)S(1)}, u32[]{:S(2)}) copy-start(f32[960]{0:T(1024)S(1)} %get-tuple-element.133) | copy-start | bytes 11524
  828.6 205.1 %copy-start.1 = (bf16[1,1536,768]{2,1,0:T(8,128)(2,1)S(1)}, bf16[1,1536,768]{2,1,0:T(8,128)(2,1)}, u32[]{:S(2)}) copy-start(bf16[1,1536,768]{2,1,0:T(8,128)(2,1)} %param.47) | copy-start | bytes 7077892
  (58 other events, 149.9 us)
Sparse Core Ops, SparseCore 0:
  11.4 65.2 all-gather.3
  80.1 100.1 all-gather.5
  183.7 61.2 all-gather.7
  622.1 134.6 reduce-scatter.7
  762.3 127.3 reduce-scatter.3
  894.7 137.1 reduce-scatter.5
